TPU v7x, 128 devices: a whole 4x4x4 slice. The times are simulated.
128 devices in a mesh: gz: 8 (over y, core), xy: 16 (over x, z).
Axes of the slice: x: 4, y: 4, z: 4, core: 2. Of those that a mesh axis runs over, the one named last changes fastest.
Arguments:
- density: float32 [256, 512, 1024], P('gz', 'xy')
- uptake: float32 [256, 512, 1024], P('gz', 'xy'), may hold values from 0.5 to 50
- brick_values: bfloat16 [9216, 4096], P(('gz', 'xy'))
- brick_ids: int32 [9216], P(('gz', 'xy')), may hold values from 0 to 32767, as said below
- slot_counts: int32 [128, 9], P(('gz', 'xy')), may hold values from 0 to 8, as said below
Outputs:
- supply: float32 [256, 512, 1024], P('gz', 'xy')
- concentration: float32 [256, 512, 1024], P('gz', 'xy')
Inputs may be any that keep to these rules, and one draw needn't show every extreme that they name: `brick_ids`: the slots 8 j to 8 j + 7 of each device (j = 0 to 8) name bricks of the device whose gz index differs by j // 3 - 1 and whose xy index differs by j % 3 - 1, or of the device itself where no such device exists; the first and the last brick of the grid are both named. `slot_counts`: entry j of a device counts the live slots at the start of its block j; it is 0 where block j's device does not exist, and 8 for j = 4.
All inputs are finite; a program needn't handle non-finite values.
Results may differ from a plain program's by a relative error of at most 0.0014.
Values may be sent and summed in bfloat16 or wider, within the bound.
A program may use at most 576 MiB of HBM per device.

v0:
```python
import jax
import jax.numpy as jnp
from jax import lax
from jax.sharding import PartitionSpec as P

EDGE = 16
CAP = 8
LEVELS = 4
NU = 2
NC = 4
BRICK = 4096
SLOTS = 72


KAPPA = 32.0
OMEGA = 0.8


def extended(shard, sides, width):
    for axis, dim in sides:
        count, length = (lax.axis_size(axis), shard.shape[dim])
        up = [(i, (i + 1) % count) for i in range(count - 1)]
        down = [(j, i) for i, j in up]
        last = lax.slice_in_dim(shard, length - width, length, axis=dim)
        initial = lax.slice_in_dim(shard, 0, width, axis=dim)
        before = lax.ppermute(last, axis, up)
        after = lax.ppermute(initial, axis, down)
        shard = jnp.concatenate([before, shard, after], axis=dim)
    return shard


def from_behind(block, axis, distance):
    devices = range(lax.axis_size(axis))
    route = [(i - distance, i) for i in devices if i - distance in devices]
    return lax.ppermute(block, axis, route)


def as_sent(shard):
    return jax.tree.map(lambda a: a.astype(jnp.bfloat16) if a.dtype == jnp.float32 else a, shard)


def neighbours(padded, values):
    y_padded = jnp.pad(values, ((0, 0), (0, 0), (1, 1)))
    summed = padded[2:, 1:-1] + padded[:-2, 1:-1]
    summed = summed + padded[1:-1, 2:] + padded[1:-1, :-2]
    summed = summed + y_padded[:, :, 2:] + y_padded[:, :, :-2]
    return summed


def operate(values, diagonal, spread):
    padded = extended(values, (("gz", 0), ("xy", 1)), 1)
    return diagonal * values - spread * neighbours(padded, values)


def smooth_once(values, source, diagonal, spread):
    return values + OMEGA * (source - operate(values, diagonal, spread)) / diagonal


def shrink(values):
    zsize, xsize, ysize = values.shape
    return values.reshape(zsize // 2, 2, xsize // 2, 2, ysize // 2, 2).mean(axis=(1, 3, 5))


def expand(values):
    return jnp.repeat(jnp.repeat(jnp.repeat(values, 2, 0), 2, 1), 2, 2)


def descend(level_index, source, start, rates):
    spread = KAPPA / 4.0**level_index
    diagonal = 1.0 + rates + 6.0 * spread
    estimate = start
    if level_index == LEVELS - 1:
        for repeat in range(NC):
            estimate = smooth_once(estimate, source, diagonal, spread)
        return estimate
    for repeat in range(NU):
        estimate = smooth_once(estimate, source, diagonal, spread)
    remainder = source - operate(estimate, diagonal, spread)
    coarser = shrink(remainder)
    update = descend(level_index + 1, coarser, jnp.zeros_like(coarser), shrink(rates))
    estimate = estimate + expand(update)
    for repeat in range(NU):
        estimate = smooth_once(estimate, source, diagonal, spread)
    return estimate


def slab_step(labels, payload, offset):
    return from_behind((labels, payload), "gz", offset)


def tile_step(labels, payload, offset):
    return (
        from_behind(as_sent(labels), "xy", offset).astype(labels.dtype),
        from_behind(payload, "xy", offset),
    )


def shards(density, uptake, brick_values, brick_ids, slot_counts):
    depth_z, width_x, length_y = density.shape
    per_z = depth_z // EDGE
    per_x = width_x // EDGE
    per_y = length_y // EDGE
    tiles = lax.axis_size("xy")
    bricks_x = per_x * tiles
    within = jnp.arange(SLOTS, dtype=jnp.int32)
    is_live = within % CAP < slot_counts[0, within // CAP]
    masked = jnp.where(is_live[:, None], brick_values, jnp.zeros_like(brick_values))
    value_grid = masked.reshape(3, 3, CAP, BRICK)
    label_grid = brick_ids.reshape(3, 3, CAP)
    first_hop = {}
    for offset in (1, -1):
        first_hop[offset] = slab_step(label_grid[offset + 1], value_grid[offset + 1], offset)
    held_ids = jnp.concatenate([label_grid[1], first_hop[1][0], first_hop[-1][0]], axis=1)
    held_values = jnp.concatenate([value_grid[1], first_hop[1][1], first_hop[-1][1]], axis=1)
    second_hop = {}
    for offset in (1, -1):
        second_hop[offset] = tile_step(held_ids[offset + 1], held_values[offset + 1], offset)
    arrived_ids = jnp.concatenate([held_ids[1], second_hop[1][0], second_hop[-1][0]], axis=0)
    arrived = jnp.concatenate([held_values[1], second_hop[1][1], second_hop[-1][1]], axis=0)
    brick_y = arrived_ids % per_y
    rest_ids = arrived_ids // per_y
    brick_x = rest_ids % bricks_x
    brick_z = rest_ids // bricks_x
    local_brick = (brick_z % per_z * per_x + brick_x % per_x) * per_y + brick_y
    one_hot = (
        local_brick[None, :] == jnp.arange(per_z * per_x * per_y, dtype=jnp.int32)[:, None]
    ).astype(jnp.bfloat16)
    gathered = jnp.dot(one_hot, arrived, preferred_element_type=jnp.float32)
    secretion = (
        gathered.reshape(per_z, per_x, per_y, EDGE, EDGE, EDGE)
        .transpose(0, 3, 1, 4, 2, 5)
        .reshape(depth_z, width_x, length_y)
    )
    supply = density + secretion
    concentration = descend(0, supply, density, uptake)
    return (supply, concentration)


def solution(mesh):
    return jax.shard_map(
        shards,
        mesh=mesh,
        in_specs=(
            P("gz", "xy", None),
            P("gz", "xy", None),
            P(("gz", "xy"), None),
            P(("gz", "xy")),
            P(("gz", "xy"), None),
        ),
        out_specs=(P("gz", "xy", None), P("gz", "xy", None)),
        check_vma=False,
    )
```

profile of v0, /device:TPU:30, one launch (start us, length us, event | category | flops | bytes accessed | tf_op | source)
XLA Modules:
  0.0 1377.0 jit_solution(1229468145017972888)
XLA Ops:
  34.9 6.0 collective-permute-start.7
  49.9 9.3 reshape.351
  59.2 24.0 %copy.99 = f32[2,16,2,16,64,16]{5,4,3,2,1,0:T(8,128)} copy(f32[2,16,2,16,64,16]{4,2,0,5,3,1:T(2,128)} %bitcast.37) | data formatting | bytes 8388608 | tf_op jit(solution)/shard_map/transpose | solution.py:131
  83.2 28.3 %reshape.352 = f32[32,32,1024]{2,1,0:T(8,128)} reshape(f32[2,16,2,16,64,16]{5,4,3,2,1,0:T(8,128)} %copy.99) | data formatting | bytes 8388608 | tf_op jit(solution)/shard_map/reshape | solution.py:132
  111.5 17.3 %fusion.7 = (f32[32,32,1024]{2,1,0:T(8,128)}, f32[32,32,1024]{2,1,0:T(8,128)S(1)}) fusion(f32[32,32,1024]{2,1,0:T(8,128)} %param.5, f32[34,32,1024]{2,1,0:T(8,128)} %copy-done.8, f32[34,1,1024]{2,1,0:T(1,128)S(1)} %collective-permute-done.11, f32[34,1,1024]{2,1,0:T(1,128)S(1)} %collective-permute-done.10, f32[1,32,1024]{2,1,0:T(8,128)S(1)} %collective-permute-done.9, ...), kind=kLoop, calls=%fused_computation.18 | loop fusion | flops 18874368 | bytes 25968640 | tf_op jit(solution)/shard_map/add | solution.py:56
  149.3 6.5 collective-permute-done.15
  155.8 18.8 %fusion.15 = f32[32,32,1024]{2,1,0:T(8,128)} fusion(f32[32,32,1024]{2,1,0:T(8,128)} %get-tuple-element.2, f32[32,32,1024]{2,1,0:T(8,128)S(1)} %get-tuple-element.3, f32[34,1,1024]{2,1,0:T(1,128)S(1)} %collective-permute-done.15, f32[1,32,1024]{2,1,0:T(8,128)S(1)} %collective-permute-done.12, f32[1,32,1024]{2,1,0:T(8,128)S(1)} %collective-permute-done.13, ...), kind=kLoop, calls=%fused_computation.26 | loop fusion | flops 22020096 | bytes 17317888 | tf_op jit(solution)/shard_map/add | solution.py:56
  194.7 270.4 %reshape.354 = f32[16,2,16,2,512,2]{5,4,3,2,1,0:T(8,128)} reshape(f32[32,32,1024]{2,1,0:T(8,128)} %param.6) | data formatting | bytes 8388608 | tf_op jit(solution)/shard_map/reshape | solution.py:61
  465.1 81.0 %reduce_sum.55 = f32[16,16,512]{2,1,0:T(8,128)} reduce(f32[16,2,16,2,512,2]{5,4,3,2,1,0:T(8,128)} %reshape.354, f32[]{:T(128)} %constant.132.clone.1), dimensions={1,3,5}, to_apply=%region_1.2 | reduce | flops 917504 | bytes 4718596 | tf_op jit(solution)/shard_map/reduce_sum | solution.py:61
  554.7 21.3 %fusion.20 = f32[32,32,1024]{2,1,0:T(8,128)} fusion(f32[32,32,1024]{2,1,0:T(8,128)} %copy-done.4, f32[32,32,1024]{2,1,0:T(8,128)} %fusion.15, f32[34,1,1024]{2,1,0:T(1,128)} %collective-permute-done.19, f32[1,32,1024]{2,1,0:T(8,128)S(1)} %copy-done.12, f32[1,32,1024]{2,1,0:T(8,128)S(1)} %copy-done.14, f32[34,1,1024]{2,1,0:T(1,128)} %collective-permute-done.18, ...), kind=kLoop, calls=%fused_computation.31 | loop fusion | flops 18874368 | bytes 17317888 | tf_op jit(solution)/shard_map/sub | solution.py:78
  576.0 270.4 %reshape.353 = f32[16,2,16,2,512,2]{5,4,3,2,1,0:T(8,128)} reshape(f32[32,32,1024]{2,1,0:T(8,128)} %fusion.20) | data formatting | bytes 8388608 | tf_op jit(solution)/shard_map/reshape | solution.py:61
  846.3 80.2 %reduce_sum.54 = f32[16,16,512]{2,1,0:T(8,128)S(1)} reduce(f32[16,2,16,2,512,2]{5,4,3,2,1,0:T(8,128)} %reshape.353, f32[]{:T(128)} %constant.132.clone.1), dimensions={1,3,5}, to_apply=%region_0.1 | reduce | flops 917504 | bytes 4718596 | tf_op jit(solution)/shard_map/reduce_sum | solution.py:61
  936.3 5.8 collective-permute-start.26
  944.0 6.0 collective-permute-done.27
  972.6 34.9 %reshape.355 = f32[8,2,8,2,256,2]{5,4,3,2,1,0:T(8,128)} reshape(f32[16,16,512]{2,1,0:T(8,128)S(1)} %get-tuple-element.45) | data formatting | bytes 1048576 | tf_op jit(solution)/shard_map/reshape | solution.py:61
  1007.4 12.2 reduce_sum.56
  1019.6 34.9 %div.115 = f32[8,2,8,2,256,2]{5,4,3,2,1,0:T(8,128)} reshape(f32[16,16,512]{2,1,0:T(8,128)S(1)} %get-tuple-element.44) | data formatting | bytes 1048576 | tf_op jit(solution)/shard_map/div | solution.py:61
  1054.5 12.2 reduce_sum.57
  1074.9 5.8 collective-permute-start.38
  1261.6 7.7 copy.107
  1269.3 11.8 broadcast_in_dim.65
  1281.1 11.4 copy.108
  1317.1 18.8 %fusion.28 = f32[32,32,1024]{2,1,0:T(8,128)} fusion(f32[32,32,1024]{2,1,0:T(8,128)} %copy-done.6, f32[32,32,1024]{2,1,0:T(8,128)S(1)} %copy-done.5, f32[34,1,1024]{2,1,0:T(1,128)S(1)} %collective-permute-done.79, f32[1,32,1024]{2,1,0:T(8,128)S(1)} %collective-permute-done.76, f32[1,32,1024]{2,1,0:T(8,128)S(1)} %collective-permute-done.77, ...), kind=kLoop, calls=%fused_computation.39 | loop fusion | flops 22020096 | bytes 17317888 | tf_op jit(solution)/shard_map/add | solution.py:56
  1357.9 18.9 %fusion.36 = f32[32,32,1024]{2,1,0:T(8,128)} fusion(f32[32,32,1024]{2,1,0:T(8,128)} %fusion.28, f32[32,32,1024]{2,1,0:T(8,128)S(1)} %copy-done.5, f32[34,1,1024]{2,1,0:T(1,128)S(1)} %collective-permute-done.83, f32[1,32,1024]{2,1,0:T(8,128)S(1)} %collective-permute-done.80, f32[1,32,1024]{2,1,0:T(8,128)S(1)} %collective-permute-done.81, ...), kind=kLoop, calls=%fused_computation.47 | loop fusion | flops 22020096 | bytes 17317888 | tf_op jit(solution)/shard_map/add | solution.py:56
  (290 shorter events, 360.7 us)
Async XLA Ops:
  1.6 17.0 %collective-permute-start = (s32[3,8]{1,0:T(4,128)S(1)}, s32[3,8]{1,0:T(4,128)S(1)}, u32[]{:S(2)}, u32[]{:S(2)}) collective-permute-start(s32[3,8]{1,0:T(4,128)S(1)} %squeeze.35), channel_id=1, source_target_pairs={{0,16},{16,32},{32,48},{48,64},{64,80},{80,96},{96,112},{1,17},{17... | collective-permute-start | bytes 296 | tf_op jit(solution)/shard_map/ppermute | solution.py:35
  3.6 15.0 %collective-permute-start.1 = (s32[3,8]{1,0:T(4,128)S(1)}, s32[3,8]{1,0:T(4,128)S(1)}, u32[]{:S(2)}, u32[]{:S(2)}) collective-permute-start(s32[3,8]{1,0:T(4,128)S(1)} %squeeze.36), channel_id=1, source_target_pairs={{16,0},{32,16},{48,32},{64,48},{80,64},{96,80},{112,96},{17,1},{33... | collective-permute-start | bytes 296 | tf_op jit(solution)/shard_map/ppermute | solution.py:35
  10.0 22.9 %collective-permute-start.4 = (bf16[3,8,4096]{2,1,0:T(8,128)(2,1)S(1)}, bf16[3,8,4096]{2,1,0:T(8,128)(2,1)S(1)}, u32[]{:S(2)}, u32[]{:S(2)}) collective-permute-start(bf16[3,8,4096]{2,1,0:T(8,128)(2,1)S(1)} %get-tuple-element.39), channel_id=1, source_target_pairs={{0,16},{16,32},{32,48},{48,64},{64,80},{80,96},{96,112},{1,17},{17... | collective-permute-start | bytes 589832 | tf_op jit(solution)/shard_map/ppermute | solution.py:35
  11.9 21.0 %collective-permute-start.5 = (bf16[3,8,4096]{2,1,0:T(8,128)(2,1)S(1)}, bf16[3,8,4096]{2,1,0:T(8,128)(2,1)S(1)}, u32[]{:S(2)}, u32[]{:S(2)}) collective-permute-start(bf16[3,8,4096]{2,1,0:T(8,128)(2,1)S(1)} %get-tuple-element.38), channel_id=1, source_target_pairs={{16,0},{32,16},{48,32},{64,48},{80,64},{96,80},{112,96},{17,1},{33... | collective-permute-start | bytes 589832 | tf_op jit(solution)/shard_map/ppermute | solution.py:35
  16.6 13.7 collective-permute-start.9
  33.0 14.1 %collective-permute-start.6 = (bf16[24,4096]{1,0:T(8,128)(2,1)S(1)}, bf16[24,4096]{1,0:T(8,128)(2,1)S(1)}, u32[]{:S(2)}, u32[]{:S(2)}) collective-permute-start(bf16[24,4096]{1,0:T(8,128)(2,1)S(1)} %get-tuple-element.36), channel_id=1, source_target_pairs={{0,1},{1,2},{2,3},{3,4},{4,5},{5,6},{6,7},{7,8},{8,9},{9,10},{10,1... | collective-permute-start | bytes 589832 | tf_op jit(solution)/shard_map/ppermute | solution.py:35
  34.9 12.2 collective-permute-start.7
  41.2 70.3 %collective-permute-start.10 = (f32[34,1,1024]{2,1,0:T(1,128)S(1)}, f32[34,1,1024]{2,1,0:T(1,128)S(1)}, u32[]{:S(2)}, u32[]{:S(2)}) collective-permute-start(f32[34,1,1024]{2,1,0:T(1,128)S(1)} %get-tuple-element.12), channel_id=1, source_target_pairs={{1,0},{2,1},{3,2},{4,3},{5,4},{6,5},{7,6},{8,7},{9,8},{10,9},{11,1... | collective-permute-start | bytes 417800 | tf_op jit(solution)/shard_map/ppermute | solution.py:27
  43.3 68.3 %collective-permute-start.11 = (f32[34,1,1024]{2,1,0:T(1,128)S(1)}, f32[34,1,1024]{2,1,0:T(1,128)S(1)}, u32[]{:S(2)}, u32[]{:S(2)}) collective-permute-start(f32[34,1,1024]{2,1,0:T(1,128)S(1)} %get-tuple-element.13), channel_id=1, source_target_pairs={{0,1},{1,2},{2,3},{3,4},{4,5},{5,6},{6,7},{7,8},{8,9},{9,10},{10,1... | collective-permute-start | bytes 417800 | tf_op jit(solution)/shard_map/ppermute | solution.py:26
  180.6 365.5 %collective-permute-start.20 = (f32[1,16,512]{2,1,0:T(8,128)}, f32[1,16,512]{2,1,0:T(8,128)}, u32[]{:S(2)}, u32[]{:S(2)}) collective-permute-start(f32[1,16,512]{2,1,0:T(8,128)} %broadcast.350), channel_id=1, source_target_pairs={{16,0},{32,16},{48,32},{64,48},{80,64},{96,80},{112,96},{17,1},{33... | collective-permute-start | bytes 98312 | tf_op jit(solution)/shard_map/ppermute | solution.py:27
  183.8 362.4 %collective-permute-start.21 = (f32[1,16,512]{2,1,0:T(8,128)}, f32[1,16,512]{2,1,0:T(8,128)}, u32[]{:S(2)}, u32[]{:S(2)}) collective-permute-start(f32[1,16,512]{2,1,0:T(8,128)} %broadcast.350), channel_id=1, source_target_pairs={{0,16},{16,32},{32,48},{48,64},{64,80},{80,96},{96,112},{1,17},{17... | collective-permute-start | bytes 98312 | tf_op jit(solution)/shard_map/ppermute | solution.py:26
  188.9 365.7 %collective-permute-start.18 = (f32[34,1,1024]{2,1,0:T(1,128)}, f32[34,1,1024]{2,1,0:T(1,128)}, u32[]{:S(2)}, u32[]{:S(2)}) collective-permute-start(f32[34,1,1024]{2,1,0:T(1,128)} %get-tuple-element.8), channel_id=1, source_target_pairs={{1,0},{2,1},{3,2},{4,3},{5,4},{6,5},{7,6},{8,7},{9,8},{10,9},{11,1... | collective-permute-start | bytes 417800 | tf_op jit(solution)/shard_map/ppermute | solution.py:27
  190.8 363.8 %collective-permute-start.19 = (f32[34,1,1024]{2,1,0:T(1,128)}, f32[34,1,1024]{2,1,0:T(1,128)}, u32[]{:S(2)}, u32[]{:S(2)}) collective-permute-start(f32[34,1,1024]{2,1,0:T(1,128)} %get-tuple-element.9), channel_id=1, source_target_pairs={{0,1},{1,2},{2,3},{3,4},{4,5},{5,6},{6,7},{7,8},{8,9},{9,10},{10,1... | collective-permute-start | bytes 417800 | tf_op jit(solution)/shard_map/ppermute | solution.py:26
  548.5 378.1 %collective-permute-start.22 = (f32[18,1,512]{2,1,0:T(1,128)}, f32[18,1,512]{2,1,0:T(1,128)}, u32[]{:S(2)}, u32[]{:S(2)}) collective-permute-start(f32[18,1,512]{2,1,0:T(1,128)} %get-tuple-element.32), channel_id=1, source_target_pairs={{1,0},{2,1},{3,2},{4,3},{5,4},{6,5},{7,6},{8,7},{9,8},{10,9},{11,1... | collective-permute-start | bytes 110600 | tf_op jit(solution)/shard_map/ppermute | solution.py:27
  552.5 374.1 %collective-permute-start.23 = (f32[18,1,512]{2,1,0:T(1,128)}, f32[18,1,512]{2,1,0:T(1,128)}, u32[]{:S(2)}, u32[]{:S(2)}) collective-permute-start(f32[18,1,512]{2,1,0:T(1,128)} %get-tuple-element.33), channel_id=1, source_target_pairs={{0,1},{1,2},{2,3},{3,4},{4,5},{5,6},{6,7},{7,8},{8,9},{9,10},{10,1... | collective-permute-start | bytes 110600 | tf_op jit(solution)/shard_map/ppermute | solution.py:26
  955.0 11.0 collective-permute-start.32
  960.2 11.9 collective-permute-start.30
  966.1 100.6 %collective-permute-start.34 = (f32[10,1,256]{2,1,0:T(1,128)S(1)}, f32[10,1,256]{2,1,0:T(1,128)S(1)}, u32[]{:S(2)}, u32[]{:S(2)}) collective-permute-start(f32[10,1,256]{2,1,0:T(1,128)S(1)} %get-tuple-element.58), channel_id=1, source_target_pairs={{1,0},{2,1},{3,2},{4,3},{5,4},{6,5},{7,6},{8,7},{9,8},{10,9},{11,1... | collective-permute-start | bytes 30728 | tf_op jit(solution)/shard_map/ppermute | solution.py:27
  970.1 96.6 %collective-permute-start.35 = (f32[10,1,256]{2,1,0:T(1,128)S(1)}, f32[10,1,256]{2,1,0:T(1,128)S(1)}, u32[]{:S(2)}, u32[]{:S(2)}) collective-permute-start(f32[10,1,256]{2,1,0:T(1,128)S(1)} %get-tuple-element.59), channel_id=1, source_target_pairs={{0,1},{1,2},{2,3},{3,4},{4,5},{5,6},{6,7},{7,8},{8,9},{9,10},{10,1... | collective-permute-start | bytes 30728 | tf_op jit(solution)/shard_map/ppermute | solution.py:26
  1092.8 11.0 collective-permute-start.44
  1098.0 12.3 collective-permute-start.42
  1099.9 10.4 collective-permute-start.43
  1103.9 22.7 %collective-permute-start.46 = (f32[6,1,128]{2,1,0:T(1,128)S(1)}, f32[6,1,128]{2,1,0:T(1,128)S(1)}, u32[]{:S(2)}, u32[]{:S(2)}) collective-permute-start(f32[6,1,128]{2,1,0:T(1,128)S(1)} %get-tuple-element.76), channel_id=1, source_target_pairs={{1,0},{2,1},{3,2},{4,3},{5,4},{6,5},{7,6},{8,7},{9,8},{10,9},{11,1... | collective-permute-start | bytes 9224 | tf_op jit(solution)/shard_map/ppermute | solution.py:27
  1107.9 18.6 %collective-permute-start.47 = (f32[6,1,128]{2,1,0:T(1,128)S(1)}, f32[6,1,128]{2,1,0:T(1,128)S(1)}, u32[]{:S(2)}, u32[]{:S(2)}) collective-permute-start(f32[6,1,128]{2,1,0:T(1,128)S(1)} %get-tuple-element.77), channel_id=1, source_target_pairs={{0,1},{1,2},{2,3},{3,4},{4,5},{5,6},{6,7},{7,8},{8,9},{9,10},{10,1... | collective-permute-start | bytes 9224 | tf_op jit(solution)/shard_map/ppermute | solution.py:26
  (75 other events, 900.5 us)
where the time goes:
time: 1390 us; the launch traced here: 1380 us
  local copies, waits for them, and re-layouts  738 us (53%)
  other arithmetic  304 us (22%)
  starting transfers between devices  235 us (17%)
  waiting for transfers between devices  94.6 us (7%)
    reshape x4, local copies, waits for them, and re-layouts, shrink(): values.reshape(zsize // 2, 2, xsize // 2, 2, ysize // 2, 2)  581 us
    reduce_sum x6, other arithmetic, shrink(): values.reshape(zsize // 2, 2, xsize // 2, 2, ysize // 2, 2)  191 us
    ppermute x38, starting transfers between devices, extended(): after = lax.ppermute(initial, axis, down)  104 us
    ppermute x38, starting transfers between devices, extended(): before = lax.ppermute(last, axis, up)  103 us
    ppermute x38, waiting for transfers between devices, extended(): before = lax.ppermute(last, axis, up)  91.1 us
    add x13, other arithmetic, smooth_once(): values + OMEGA * (source - operate(values, diagonal, spread)) / diagonal  76 us
    div x2, local copies, waits for them, and re-layouts, shrink(): values.reshape(zsize // 2, 2, xsize // 2, 2, ysize // 2, 2)  40.4 us
    reshape x1, local copies, waits for them, and re-layouts, shards(): secretion = gathered.reshape(per_z, per_x, per_y, EDGE, EDGE, EDGE).trans...  28.3 us
  transfers between devices with their start and end apart: 84, of which 30 were waited for; matrix products, arithmetic and copies ran while one was open for 66% of the time, Pallas kernels for 0%

commit v1 on v0

v1 whole, which is shorter than its diff:
```python
import jax
import jax.numpy as jnp
from jax import lax
from jax.experimental import pallas as pl
from jax.experimental.pallas import tpu as pltpu
from jax.sharding import PartitionSpec as P

CAP = 8
BRICK = 4096
SLOTS = 72
KAPPA = (32.0, 8.0, 2.0, 0.5)
OMEGA = 0.8
LANES = 128

NZ = (32, 16, 8, 4)
NX = (32, 16, 8, 4)
NK = (8, 4, 2, 1)
HALO = (1, 3, 3, 4)
NR = (32, 24, 16, 16)
ZO = (1, 4, 4, 5)
XO = (8, 11, 11, 12)
ROWS = (48, 40, 32, 32)
PLANES = tuple(n + 2 * o for n, o in zip(NZ, ZO))

FACES = ((-1, 0), (1, 0), (0, -1), (0, 1))
AROUND = tuple((dz, dx) for dz in (-1, 0, 1) for dx in (-1, 0, 1) if dz or dx)

f32 = jnp.float32
bf16 = jnp.bfloat16


def level_shape(level):
    return (PLANES[level], NK[level], ROWS[level], LANES)


def kernel(
    dens, upt, bricks, ids, counts, out_s, out_c,
    V0, V1, V2, F0, W0, U0,
    F1, W1, D1, A1, B1, C1,
    F2, W2, D2, A2, B2, C2,
    F3, W3, A3, B3,
    RT1, RT2, RS, EB, PB, PM, EM,
    BV, XA, XT, VS, VR, IS, IR, RK, MB, TB,
    load_sem, out_sem, send_sem, recv_sem,
):
    gz, xy = lax.axis_index("gz"), lax.axis_index("xy")
    nz_dev, nx_dev = lax.axis_size("gz"), lax.axis_size("xy")
    one = jnp.minimum(gz, 0)
    taken = [0]

    def exists(dz, dx):
        ok = None
        for at, d, n in ((gz, dz, nz_dev), (xy, dx, nx_dev)):
            if d:
                cond = (at + d >= 0) & (at + d < n)
                ok = cond if ok is None else ok & cond
        return ok

    def loop(n, body, unroll=1):
        def step(i, c):
            body(i)
            return c

        lax.fori_loop(0, n, step, 0, unroll=unroll)

    class Exchange:
        def __init__(self, parts):
            self.parts = []
            for d, src, dst in parts:
                self.parts.append((d, src, dst, taken[0]))
                taken[0] += 1

        def _copy(self, d, src, dst, at):
            return pltpu.make_async_remote_copy(
                src_ref=src, dst_ref=dst, send_sem=send_sem.at[at], recv_sem=recv_sem.at[at],
                device_id=(gz + d[0], xy + d[1]), device_id_type=pl.DeviceIdType.MESH,
            )

        def start(self):
            for d, src, dst, at in self.parts:
                @pl.when(exists(*d))
                def _(d=d, src=src, dst=dst, at=at):
                    self._copy(d, src, dst, at).start()

        def wait_recv(self):
            for d, src, dst, at in self.parts:
                @pl.when(exists(-d[0], -d[1]))
                def _(d=d, src=src, dst=dst, at=at):
                    self._copy(d, src, dst, at).wait_recv()

        def wait_send(self):
            for d, src, dst, at in self.parts:
                @pl.when(exists(*d))
                def _(d=d, src=src, dst=dst, at=at):
                    self._copy(d, src, dst, at).wait_send()

    def halo_exchange(level, ref, width, directions):
        def cut(d, first, n):
            if d == 0:
                return (first, n), (first, n)
            if d > 0:
                return (first + n - width, width), (first - width, width)
            return (first, width), (first + n, width)

        parts = []
        for dz, dx in directions:
            zs, zd = cut(dz, ZO[level], NZ[level])
            xs, xd = cut(dx, XO[level], NX[level])
            parts.append((
                (dz, dx),
                ref.at[pl.ds(*zs), :, pl.ds(*xs), :],
                ref.at[pl.ds(*zd), :, pl.ds(*xd), :],
            ))
        return Exchange(parts)

    def load(src, dst_of, base):
        copies = []
        for k in range(8):
            c = pltpu.make_async_copy(
                src.at[:, :, pl.ds(k * LANES, LANES)], dst_of(k), load_sem.at[base + k]
            )
            c.start()
            copies.append(c)
        return copies

    brick_load = pltpu.make_async_copy(bricks, BV, load_sem.at[16])
    brick_load.start()
    dens_loads = load(dens, lambda k: V0.at[pl.ds(1, 32), k, pl.ds(8, 32), :], 0)
    upt_loads = load(upt, lambda k: U0.at[:, k], 8)

    def clear(ref):
        shape = ref.shape[1:]
        def body(i):
            ref[i] = jnp.zeros(shape, ref.dtype)
        loop(ref.shape[0], body)

    for V in (V0, V1, V2):
        for z in (0, 33):
            V[z] = jnp.zeros((8, 48, LANES), f32)
        def edge(z, V=V):
            V[z + 1, :, 0:8, :] = jnp.zeros((8, 8, LANES), f32)
            V[z + 1, :, 40:48, :] = jnp.zeros((8, 8, LANES), f32)
        loop(32, edge)
    for ref in (F1, W1, D1, A1, B1, C1, F2, W2, D2, A2, B2, C2, F3, W3, A3, B3):
        clear(ref)
    VR[...] = jnp.zeros(VR.shape, bf16)
    IR[...] = jnp.full(IR.shape, -1, jnp.int32)
    PB[...] = jnp.zeros(PB.shape, f32)

    barrier = pltpu.get_barrier_semaphore()
    for d in AROUND:
        @pl.when(exists(*d))
        def _(d=d):
            pl.semaphore_signal(
                barrier, inc=1, device_id=(gz + d[0], xy + d[1]), device_id_type=pl.DeviceIdType.MESH
            )

    row = lax.broadcasted_iota(jnp.int32, (256, LANES), 0)
    col = lax.broadcasted_iota(jnp.int32, (256, LANES), 1)
    pair = jnp.where(row // 2 == col, 1.0, 0.0).astype(bf16)
    PM[0:256] = pair
    PM[256:512] = pair
    row = lax.broadcasted_iota(jnp.int32, (LANES, 256), 0)
    col = lax.broadcasted_iota(jnp.int32, (LANES, 256), 1)
    twice = jnp.where(col // 2 == row, 1.0, 0.0).astype(bf16)
    EM[0:128] = twice
    EM[128:256] = twice

    for j in range(9):
        for e in range(CAP):
            IS[j, e : e + 1, :] = jnp.full((1, LANES), ids[CAP * j + e], jnp.int32)
    slot = lax.broadcasted_iota(jnp.int32, (CAP, LANES), 0)
    for j in range(9):
        v = IS[j]
        local = (((v >> 11) & 1) * 2 + ((v >> 6) & 1)) * 64 + (v & 63)
        IS[j] = jnp.where(slot < counts[0, j], local, -1)

    brick_load.wait()

    def widen(k):
        v = BV[:, pl.ds(pl.multiple_of(k * LANES, LANES), LANES)].astype(f32)
        for j in range(9):
            XA[pl.ds(pl.multiple_of((j * 32 + k) * 8, 8), 8), :] = v[8 * j : 8 * j + 8]

    loop(32, widen, unroll=2)
    chunk = lax.broadcasted_iota(jnp.int32, (32, LANES), 1) // 16

    def regroup(j):
        xs = [XA[pl.ds(j * 256 + s, 32, stride=8), :] for s in range(8)]
        for p in (1, 2, 4):
            low = (chunk & p) == 0
            for s in range(8):
                if s & p == 0:
                    a, b = xs[s], xs[s | p]
                    xs[s] = jnp.where(low, a, pltpu.roll(b, 16 * p, 1))
                    xs[s | p] = jnp.where(low, pltpu.roll(a, LANES - 16 * p, 1), b)
        for t in range(8):
            XT[pl.ds(j * 256 + t, 32, stride=8), :] = xs[t]
        VS[j] = XT[pl.ds(pl.multiple_of(j * 256, 256), 256), :].astype(bf16)

    loop(9, regroup)
    VR[:, 4 * LANES : 5 * LANES] = VS[4]
    IR[4] = IS[4]

    def beside(at, n):
        return 1 + jnp.where(at > 0, 1, 0) + jnp.where(at < n - 1, 1, 0)

    pl.semaphore_wait(barrier, beside(gz, nz_dev) * beside(xy, nx_dev) - 1)

    parts = []
    for dz, dx in AROUND:
        j = (dz + 1) * 3 + dx + 1
        parts.append(((dz, dx), VS.at[j], VR.at[:, pl.ds(j * LANES, LANES)]))
        parts.append(((dz, dx), IS.at[j], IR.at[j]))
    send_bricks = Exchange(parts)
    send_bricks.start()
    started = [send_bricks]

    def send(level, ref, width, directions):
        e = halo_exchange(level, ref, width, directions)
        e.start()
        started.append(e)
        return e

    for c in dens_loads:
        c.wait()
    x_dens = send(0, V0, 1, FACES)

    for c in upt_loads:
        c.wait()

    def weights0(z):
        for k in range(8):
            W0[z, k] = (OMEGA * KAPPA[0]) / (1.0 + 6.0 * KAPPA[0] + U0[z, k])

    loop(32, weights0)

    def split(x):
        hi = x.astype(bf16)
        return hi, (x - hi.astype(f32)).astype(bf16)

    def restrict(level, planes, store, first):
        rows = NX[level] // 2
        step = max(8, rows)
        def gather(z1):
            for k, v in enumerate(planes(z1)):
                n = v.shape[0]
                RS[k, 0:n, :] = v
                s = RS[k, pl.ds(first, rows, stride=2), :] + RS[k, pl.ds(first + 1, rows, stride=2), :]
                EB[k // 2, k % 2, pl.ds(pl.multiple_of(z1 * step, step), rows), :] = s
        loop(NZ[level] // 2, gather)
        n = NZ[level] // 2 * step
        for k1 in range(NK[level] // 2):
            x = jnp.concatenate([EB[k1, 0, 0:n, :], EB[k1, 1, 0:n, :]], axis=1)
            hi, lo = split(x)
            y = jnp.dot(jnp.concatenate([hi, lo], axis=1), PM[...], preferred_element_type=f32)
            for z1 in range(NZ[level] // 2):
                store(z1, k1, y[z1 * step : z1 * step + rows])

    EB[...] = jnp.zeros(EB.shape, f32)

    def store_rates(level, D, W, RT):
        def store(z1, k1, s):
            rates = 0.125 * s
            kappa = KAPPA[level]
            d = (1.0 + 6.0 * kappa + rates) * (1.0 / kappa)
            n = NX[level]
            W[ZO[level] + z1, k1, pl.ds(XO[level], n), :] = OMEGA / d
            if D is not None:
                D[ZO[level] + z1, k1, pl.ds(XO[level], n), :] = d
            if RT is not None:
                RT[z1, k1, 0:n, :] = rates
        return store

    restrict(0, lambda z1: [U0[2 * z1, k] + U0[2 * z1 + 1, k] for k in range(8)], store_rates(1, D1, W1, RT1), 0)
    restrict(1, lambda z1: [RT1[2 * z1, k] + RT1[2 * z1 + 1, k] for k in range(4)], store_rates(2, D2, W2, RT2), 0)
    restrict(2, lambda z1: [RT2[2 * z1, k] + RT2[2 * z1 + 1, k] for k in range(2)], store_rates(3, None, W3, None), 0)
    x_w1 = send(1, W1, HALO[1], AROUND)
    x_w2 = send(2, W2, HALO[2], AROUND)
    x_w3 = send(3, W3, HALO[3], AROUND)

    send_bricks.wait_recv()
    inner = lax.broadcasted_iota(jnp.int32, (16, LANES), 0)

    def keys(j):
        for s in range(8):
            r = jnp.broadcast_to(IR[j, s : s + 1, :], (16, LANES))
            RK[pl.ds(pl.multiple_of(j * 128 + s * 16, 16), 16), :] = jnp.where(r < 0, -1, r * 16 + inner)

    loop(9, keys)
    lane = lax.broadcasted_iota(jnp.int32, (LANES, LANES), 1)

    def secrete(i):
        def one_hot(j):
            at = pl.ds(pl.multiple_of(j * 128, 128), 128)
            key = RK[at, :]
            for half in range(2):
                hit = key == lane + (i * 256 + half * 128)
                MB[at, half * 128 : half * 128 + 128] = jnp.where(hit, 1.0, 0.0).astype(bf16)
        loop(9, one_hot)
        TB[...] = jnp.dot(VR[...], MB[...], preferred_element_type=f32)
        g = i // 4
        bz, bx, kk = g // 2, g % 2, i % 4
        def place(a):
            z = bz * 16 + a
            for half in range(2):
                k = 2 * kk + half
                x = pl.multiple_of(8 + bx * 16, 8)
                t = TB[pl.ds(pl.multiple_of(a * 16, 16), 16), half * 128 : half * 128 + 128]
                s = V0[z + 1, k, pl.ds(x, 16), :] + t
                V2[z + 1, k, pl.ds(x, 16), :] = s
                F0[z, k, pl.ds(pl.multiple_of(bx * 16, 8), 16), :] = s * (1.0 / KAPPA[0])
        loop(16, place, unroll=4)

    loop(16, secrete)
    supply_out = []
    for k in range(8):
        c = pltpu.make_async_copy(
            V2.at[pl.ds(1, 32), k, pl.ds(8, 32), :], out_s.at[:, :, pl.ds(k * LANES, LANES)], out_sem.at[k]
        )
        c.start()
        supply_out.append(c)

    def neighbours(ref, z, first, n, nk):
        lane = lax.broadcasted_iota(jnp.int32, (n, LANES), 1)
        at_first, at_last = lane == 0, lane == LANES - 1
        centre = [ref[z, k, pl.ds(first, n), :] for k in range(nk)]
        up = [pltpu.roll(c, 1, 1) for c in centre]
        down = [pltpu.roll(c, LANES - 1, 1) for c in centre]
        out = []
        for k in range(nk):
            before = up[k - 1] if k else jnp.zeros_like(up[k])
            after = down[k + 1] if k < nk - 1 else jnp.zeros_like(up[k])
            s = ref[z - 1, k, pl.ds(first, n), :] + ref[z + 1, k, pl.ds(first, n), :]
            s = s + ref[z, k, pl.ds(first - 1 + one, n), :] + ref[z, k, pl.ds(first + 1 + one, n), :]
            s = s + jnp.where(at_first, before, up[k]) + jnp.where(at_last, after, down[k])
            out.append((centre[k], s))
        return out

    def sweep0(dst, src):
        def body(z):
            for k, (c, s) in enumerate(neighbours(src, z + 1, 8, 32, 8)):
                dst[z + 1, k, 8:40, :] = (1.0 - OMEGA) * c + W0[z, k] * (F0[z, k] + s)
        loop(32, body)

    def sweep(level, dst, src, F, W, reach, inside=False):
        nk, n, xo, nx = NK[level], NR[level], XO[level], NX[level]
        start = ZO[level] - reach
        def body(i):
            z = start + i
            for k, (c, s) in enumerate(neighbours(src, z, 8, n, nk)):
                v = (1.0 - OMEGA) * c + W[z, k, 8 : 8 + n, :] * (F[z, k, 8 : 8 + n, :] + s)
                if inside:
                    dst[z, k, xo : xo + nx, :] = v[xo - 8 : xo - 8 + nx]
                else:
                    dst[z, k, 8 : 8 + n, :] = v
        loop(NZ[level] + 2 * reach, body)

    def from_zero(level, dst, F, W):
        n = NR[level]
        start = ZO[level] - HALO[level]
        def body(i):
            z = start + i
            for k in range(NK[level]):
                dst[z, k, 8 : 8 + n, :] = W[z, k, 8 : 8 + n, :] * F[z, k, 8 : 8 + n, :]
        loop(NZ[level] + 2 * HALO[level], body)

    def residual0(z):
        out = []
        for k, (c, s) in enumerate(neighbours(V2, z + 1, 8, 32, 8)):
            d = (1.0 + 6.0 * KAPPA[0]) / KAPPA[0] + (1.0 / KAPPA[0]) * U0[z, k]
            out.append(F0[z, k] - d * c + s)
        return out

    def residual(level, ref, F, D):
        n = NR[level]
        def plane(z):
            z = z + ZO[level]
            return [
                F[z, k, 8 : 8 + n, :] - D[z, k, 8 : 8 + n, :] * c + s
                for k, (c, s) in enumerate(neighbours(ref, z, 8, n, NK[level]))
            ]
        return plane

    def coarse_source(level, plane, F, first):
        def planes(z1):
            return [a + b for a, b in zip(plane(2 * z1), plane(2 * z1 + 1))]
        def store(z1, k1, s):
            F[ZO[level + 1] + z1, k1, pl.ds(XO[level + 1], NX[level + 1]), :] = 0.5 * s
        restrict(level, planes, store, first)

    def prolong(level, dst, src, reach, rows):
        c = level + 1
        n = NR[c]
        base = XO[level] + 2 * (8 - XO[c])
        first = ZO[c] - 1
        def body(i):
            zc = first + i
            x = jnp.concatenate([src[zc, k, 8 : 8 + n, :] for k in range(NK[c])], axis=0)
            hi, lo = split(x)
            y = jnp.dot(jnp.concatenate([hi, lo], axis=1), EM[...], preferred_element_type=f32)
            for k in range(NK[level]):
                v = y[(k // 2) * n : (k // 2 + 1) * n, (k % 2) * 128 : (k % 2 + 1) * 128]
                PB[k, pl.ds(base, n, stride=2), :] = v
                PB[k, pl.ds(base + 1, n, stride=2), :] = v
            z = ZO[level] + 2 * (zc - ZO[c])
            lo_r, n_r = rows
            if level == 0:
                for k in range(NK[level]):
                    p = PB[k, pl.ds(lo_r, n_r), :]
                    @pl.when(i > 0)
                    def _():
                        dst[z, k, pl.ds(lo_r, n_r), :] = dst[z, k, pl.ds(lo_r, n_r), :] + p
                    @pl.when(i < NZ[c] + 1)
                    def _():
                        dst[z + 1, k, pl.ds(lo_r, n_r), :] = dst[z + 1, k, pl.ds(lo_r, n_r), :] + p
            else:
                for k in range(NK[level]):
                    p = PB[k, pl.ds(lo_r, n_r), :]
                    for dz in range(2):
                        dst[z + dz, k, pl.ds(lo_r, n_r), :] = dst[z + dz, k, pl.ds(lo_r, n_r), :] + p
        loop(NZ[c] + 2, body)

    x_dens.wait_recv()
    level0_sends = [x_dens]
    sweep0(V1, V0)
    x = send(0, V1, 1, FACES)
    level0_sends.append(x)
    for c in supply_out:
        c.wait()
    x.wait_recv()
    sweep0(V2, V1)
    x = send(0, V2, 1, FACES)
    level0_sends.append(x)
    x.wait_recv()
    coarse_source(0, residual0, F1, 0)

    x = send(1, F1, HALO[1], AROUND)
    x_w1.wait_recv()
    x.wait_recv()
    from_zero(1, A1, F1, W1)
    sweep(1, B1, A1, F1, W1, 2)
    coarse_source(1, residual(1, B1, F1, D1), F2, XO[1] - 8)

    x = send(2, F2, HALO[2], AROUND)
    x_w2.wait_recv()
    x.wait_recv()
    from_zero(2, A2, F2, W2)
    sweep(2, B2, A2, F2, W2, 2)
    coarse_source(2, residual(2, B2, F2, D2), F3, XO[2] - 8)

    x = send(3, F3, HALO[3], AROUND)
    x_w3.wait_recv()
    x.wait_recv()
    from_zero(3, A3, F3, W3)
    sweep(3, B3, A3, F3, W3, 3)
    sweep(3, A3, B3, F3, W3, 2)
    sweep(3, B3, A3, F3, W3, 1)

    prolong(2, B2, B3, 1, (8, NR[2]))
    sweep(2, A2, B2, F2, W2, 1)
    sweep(2, C2, A2, F2, W2, 0, inside=True)
    x = send(2, C2, 1, AROUND)
    x.wait_recv()

    prolong(1, B1, C2, 1, (8, NR[1]))
    sweep(1, A1, B1, F1, W1, 1)
    sweep(1, C1, A1, F1, W1, 0, inside=True)
    x = send(1, C1, 1, FACES)
    x.wait_recv()

    for e in level0_sends:
        e.wait_send()
        started.remove(e)
    prolong(0, V2, C1, 1, (0, 48))
    sweep0(V0, V2)
    x = send(0, V0, 1, FACES)
    x.wait_recv()
    sweep0(V1, V0)
    result_out = []
    for k in range(8):
        c = pltpu.make_async_copy(
            V1.at[pl.ds(1, 32), k, pl.ds(8, 32), :], out_c.at[:, :, pl.ds(k * LANES, LANES)], out_sem.at[8 + k]
        )
        c.start()
        result_out.append(c)
    for e in started:
        e.wait_send()
    for c in result_out:
        c.wait()


def scratch():
    def vmem(*shape, dtype=f32):
        return pltpu.VMEM(shape, dtype)

    v = [vmem(*level_shape(0)) for _ in range(3)]
    v += [vmem(32, 8, 32, LANES) for _ in range(3)]
    for level, count in ((1, 6), (2, 6), (3, 4)):
        v += [vmem(*level_shape(level)) for _ in range(count)]
    v += [
        vmem(16, 4, 16, LANES), vmem(8, 2, 8, LANES),
        vmem(8, 32, LANES),
        vmem(4, 2, 256, LANES),
        vmem(8, 56, LANES),
        vmem(512, LANES, dtype=bf16), vmem(256, 256, dtype=bf16),
        vmem(SLOTS, BRICK, dtype=bf16),
        vmem(9 * 256, LANES), vmem(9 * 256, LANES),
        vmem(9, 256, LANES, dtype=bf16), vmem(256, 9 * LANES, dtype=bf16),
        vmem(9, 8, LANES, dtype=jnp.int32), vmem(9, 8, LANES, dtype=jnp.int32),
        vmem(9 * LANES, LANES, dtype=jnp.int32),
        vmem(9 * LANES, 256, dtype=bf16), vmem(256, 256),
        pltpu.SemaphoreType.DMA((17,)), pltpu.SemaphoreType.DMA((16,)),
        pltpu.SemaphoreType.DMA((100,)), pltpu.SemaphoreType.DMA((100,)),
    ]
    return v


def shards(density, uptake, brick_values, brick_ids, slot_counts):
    any_space = pl.BlockSpec(memory_space=pl.ANY)
    smem = pl.BlockSpec(memory_space=pltpu.SMEM)
    return pl.pallas_call(
        kernel,
        out_shape=(
            jax.ShapeDtypeStruct(density.shape, f32),
            jax.ShapeDtypeStruct(density.shape, f32),
        ),
        in_specs=[any_space, any_space, any_space, smem, smem],
        out_specs=(any_space, any_space),
        scratch_shapes=scratch(),
        compiler_params=pltpu.CompilerParams(
            collective_id=0, has_side_effects=True, vmem_limit_bytes=62 * 1024 * 1024
        ),
        name="tissue_step",
    )(density, uptake, brick_values, brick_ids, slot_counts)


def solution(mesh):
    return jax.shard_map(
        shards,
        mesh=mesh,
        in_specs=(
            P("gz", "xy", None),
            P("gz", "xy", None),
            P(("gz", "xy"), None),
            P(("gz", "xy")),
            P(("gz", "xy"), None),
        ),
        out_specs=(P("gz", "xy", None), P("gz", "xy", None)),
        check_vma=False,
    )
```

time: 1390 us -> 117 us (0.08)
  local copies, waits for them, and re-layouts: 738 us -> 6.96 us
  other arithmetic: 304 us -> 0 us
  starting transfers between devices: 235 us -> 0 us
  Pallas kernels: 0 us -> 109 us
  waiting for transfers between devices: 94.6 us -> 0 us
    reshape x14 -> x0, local copies, waits for them, and re-layouts: 644 us -> none  [the longest x4 581 us: shrink(): values.reshape(zsize // 2, 2, xsize // 2, 2, ysize // 2, 2)]
    ppermute x84 -> x0, starting transfers between devices: 235 us -> none  [the longest x38 104 us: extended(): after = lax.ppermute(initial, axis, down)]
    reduce_sum x6 -> x0, other arithmetic: 191 us -> none  [shrink(): values.reshape(zsize // 2, 2, xsize // 2, 2, ysize // 2, 2)]
    pallas_call x0 -> x1, Pallas kernels: none -> 109 us  [shards(): pl.pallas_call(kernel, out_shape=(jax.ShapeDtypeStruct(density.shape, f32...]
    ppermute x84 -> x0, waiting for transfers between devices: 94.6 us -> none  [the longest x38 91.1 us: extended(): before = lax.ppermute(last, axis, up)]
    add x17 -> x0, other arithmetic: 80.7 us -> none  [the longest x13 76 us: smooth_once(): values + OMEGA * (source - operate(values, diagonal, spread)) / diagonal]
    div x2 -> x0, local copies, waits for them, and re-layouts: 40.4 us -> none  [shrink(): values.reshape(zsize // 2, 2, xsize // 2, 2, ysize // 2, 2)]
    transpose x1 -> x0, local copies, waits for them, and re-layouts: 24 us -> none  [shards(): secretion = gathered.reshape(per_z, per_x, per_y, EDGE, EDGE, EDGE).trans...]
  transfers between devices with their start and end apart: 84 -> 0, of which waited for: 30 -> 0; matrix products, arithmetic and copies ran while one was open for 66% -> 0% of each run, Pallas kernels for 0% -> 0%
where the time goes in v1:
time: 117 us; the launch traced here: 116 us
  Pallas kernels  109 us (93%)
  local copies, waits for them, and re-layouts  6.96 us (6%)
    pallas_call x1, Pallas kernels, shards(): pl.pallas_call(kernel, out_shape=(jax.ShapeDtypeStruct(density.shape, f32...  109 us
    unnamed x4, local copies, waits for them, and re-layouts  6.96 us

profile of v1, /device:TPU:30, one launch (start us, length us, event | category | flops | bytes accessed | tf_op | source)
XLA Modules:
  0.0 116.4 jit_solution(16380079545482171838)
XLA Ops:
  0.6 108.8 %tissue_step.1 = (f32[32,32,1024]{2,1,0:T(8,128)}, f32[32,32,1024]{2,1,0:T(8,128)}) custom-call(f32[32,32,1024]{2,1,0:T(8,128)} %dens.1, f32[32,32,1024]{2,1,0:T(8,128)} %upt.1, bf16[72,4096]{1,0:T(8,128)(2,1)} %bricks.1, s32[72]{0:T(128)} %ids.1, s32[1,9]{1,0:T(1,128)} %counts.1), custom_call_target="tpu_custom_call" | custom-call | tf_op jit(solution)/shard_map/tissue_step/pallas_call | solution.py:522
  109.4 0.0 copy-start
  109.4 4.9 %copy.9 = f32[32,32,1024]{2,1,0:T(8,128)} copy(f32[32,32,1024]{2,1,0:T(8,128)} %get-tuple-element.4) | data formatting | bytes 8388608
  114.3 0.0 copy-done
  114.4 2.0 %copy.10 = f32[32,32,1024]{2,1,0:T(8,128)} copy(f32[32,32,1024]{2,1,0:T(8,128)S(1)} %copy-done) | data formatting | bytes 8388608
Async XLA Ops:
  109.4 5.0 %copy-start = (f32[32,32,1024]{2,1,0:T(8,128)S(1)}, f32[32,32,1024]{2,1,0:T(8,128)}, u32[]{:S(2)}) copy-start(f32[32,32,1024]{2,1,0:T(8,128)} %get-tuple-element.5) | copy-start | bytes 12582916

commit v2 on v1

--- a/solution.py
+++ b/solution.py
@@ -41,12 +41,14 @@
     F3, W3, A3, B3,
     RT1, RT2, RS, EB, PB, PM, EM,
     BV, XA, XT, VS, VR, IS, IR, RK, MB, TB,
+    XSD, XD, XSV, XV,
     load_sem, out_sem, send_sem, recv_sem,
 ):
     gz, xy = lax.axis_index("gz"), lax.axis_index("xy")
     nz_dev, nx_dev = lax.axis_size("gz"), lax.axis_size("xy")
     one = jnp.minimum(gz, 0)
     taken = [0]
+    started = []
 
     def exists(dz, dx):
         ok = None
@@ -113,6 +115,51 @@
             ))
         return Exchange(parts)
 
+    class Faces:
+        def __init__(self, V, out, into):
+            self.rows = V.reshape(34 * 8 * 48, LANES)
+            self.out, self.into = out, into
+            inner = pl.ds(8, 32)
+            self.z = Exchange((
+                ((-1, 0), V.at[1, :, inner, :], V.at[33, :, inner, :]),
+                ((1, 0), V.at[32, :, inner, :], V.at[0, :, inner, :]),
+            ))
+            self.x = [
+                Exchange([
+                    ((0, dx), out.at[side, half], into.at[side, half])
+                    for side, dx in ((0, -1), (1, 1))
+                ])
+                for half in range(2)
+            ]
+
+        def send_x(self, half):
+            def pack(i):
+                z = half * 16 + 2 * i + 1
+                for side, row in ((0, 8), (1, 39)):
+                    v = [self.rows[pl.ds((z + p) * 384 + row, 8, stride=48), :] for p in range(2)]
+                    at = pl.ds(pl.multiple_of(i * 16, 16), 16)
+                    self.out[side, half, at, :] = jnp.concatenate(v, axis=0).astype(self.out.dtype)
+            loop(8, pack, unroll=2)
+            self.x[half].start()
+            started.append(self.x[half])
+
+        def send_z(self):
+            self.z.start()
+            started.append(self.z)
+
+        def take_x(self, half):
+            self.x[half].wait_recv()
+            def unpack(i):
+                z = half * 16 + 2 * i + 1
+                for side, row in ((0, 40), (1, 7)):
+                    v = self.into[side, half, pl.ds(pl.multiple_of(i * 16, 16), 16), :].astype(f32)
+                    for p in range(2):
+                        self.rows[pl.ds((z + p) * 384 + row, 8, stride=48), :] = v[8 * p : 8 * p + 8]
+            loop(8, unpack, unroll=2)
+
+        def take_z(self):
+            self.z.wait_recv()
+
     def load(src, dst_of, base):
         copies = []
         for k in range(8):
@@ -134,18 +181,8 @@
             ref[i] = jnp.zeros(shape, ref.dtype)
         loop(ref.shape[0], body)
 
-    for V in (V0, V1, V2):
-        for z in (0, 33):
-            V[z] = jnp.zeros((8, 48, LANES), f32)
-        def edge(z, V=V):
-            V[z + 1, :, 0:8, :] = jnp.zeros((8, 8, LANES), f32)
-            V[z + 1, :, 40:48, :] = jnp.zeros((8, 8, LANES), f32)
-        loop(32, edge)
-    for ref in (F1, W1, D1, A1, B1, C1, F2, W2, D2, A2, B2, C2, F3, W3, A3, B3):
+    for ref in (F1, W1, C1, F2, W2, C2, F3, W3):
         clear(ref)
-    VR[...] = jnp.zeros(VR.shape, bf16)
-    IR[...] = jnp.full(IR.shape, -1, jnp.int32)
-    PB[...] = jnp.zeros(PB.shape, f32)
 
     barrier = pltpu.get_barrier_semaphore()
     for d in AROUND:
@@ -154,6 +191,35 @@
             pl.semaphore_signal(
                 barrier, inc=1, device_id=(gz + d[0], xy + d[1]), device_id_type=pl.DeviceIdType.MESH
             )
+
+    def absent(dz, dx):
+        return jnp.logical_not(exists(dz, dx))
+
+    for V in (V0, V1, V2):
+        for dz, z in ((-1, 0), (1, 33)):
+            @pl.when(absent(dz, 0))
+            def _(V=V, z=z):
+                V[z, :, 8:40, :] = jnp.zeros((8, 32, LANES), f32)
+    for ref in (XD, XV):
+        for side, dx in ((0, 1), (1, -1)):
+            @pl.when(absent(0, dx))
+            def _(ref=ref, side=side):
+                for e in range(ref.shape[0]):
+                    ref[e, side] = jnp.zeros(ref.shape[2:], ref.dtype)
+    for d in AROUND:
+        j = (1 - d[0]) * 3 + 1 - d[1]
+        @pl.when(absent(*d))
+        def _(j=j):
+            VR[:, j * LANES : (j + 1) * LANES] = jnp.zeros((256, LANES), bf16)
+            IR[j] = jnp.full((CAP, LANES), -1, jnp.int32)
+    for level, refs in ((1, (A1, B1)), (2, (A2, B2)), (3, (A3, B3))):
+        shape = (NK[level], 8, LANES)
+        for ref in refs:
+            def guard(z, ref=ref, end=8 + NR[level], shape=shape):
+                ref[z, :, 0:8, :] = jnp.zeros(shape, f32)
+                ref[z, :, end : end + 8, :] = jnp.zeros(shape, f32)
+            loop(PLANES[level], guard)
+    PB[...] = jnp.zeros(PB.shape, f32)
 
     row = lax.broadcasted_iota(jnp.int32, (256, LANES), 0)
     col = lax.broadcasted_iota(jnp.int32, (256, LANES), 1)
@@ -214,7 +280,7 @@
         parts.append(((dz, dx), IS.at[j], IR.at[j]))
     send_bricks = Exchange(parts)
     send_bricks.start()
-    started = [send_bricks]
+    started.append(send_bricks)
 
     def send(level, ref, width, directions):
         e = halo_exchange(level, ref, width, directions)
@@ -224,7 +290,12 @@
 
     for c in dens_loads:
         c.wait()
-    x_dens = send(0, V0, 1, FACES)
+    faces = [Faces(V0, XSD.at[0], XD.at[0])]
+    for e, V in enumerate((V1, V2, V0)):
+        faces.append(Faces(V, XSV.at[e], XV.at[e]))
+    faces[0].send_z()
+    for half in range(2):
+        faces[0].send_x(half)
 
     for c in upt_loads:
         c.wait()
@@ -239,16 +310,21 @@
         hi = x.astype(bf16)
         return hi, (x - hi.astype(f32)).astype(bf16)
 
-    def restrict(level, planes, store, first):
+    def restrict(level, planes, store, first, halves=None):
         rows = NX[level] // 2
         step = max(8, rows)
         def gather(z1):
             for k, v in enumerate(planes(z1)):
-                n = v.shape[0]
-                RS[k, 0:n, :] = v
+                v = v if isinstance(v, list) else [v]
+                n = v[0].shape[0]
+                for x, part in enumerate(v):
+                    RS[k, x * n : (x + 1) * n, :] = part
                 s = RS[k, pl.ds(first, rows, stride=2), :] + RS[k, pl.ds(first + 1, rows, stride=2), :]
                 EB[k // 2, k % 2, pl.ds(pl.multiple_of(z1 * step, step), rows), :] = s
-        loop(NZ[level] // 2, gather)
+        if halves is None:
+            loop(NZ[level] // 2, gather)
+        else:
+            halves(gather)
         n = NZ[level] // 2 * step
         for k1 in range(NK[level] // 2):
             x = jnp.concatenate([EB[k1, 0, 0:n, :], EB[k1, 1, 0:n, :]], axis=1)
@@ -256,8 +332,6 @@
             y = jnp.dot(jnp.concatenate([hi, lo], axis=1), PM[...], preferred_element_type=f32)
             for z1 in range(NZ[level] // 2):
                 store(z1, k1, y[z1 * step : z1 * step + rows])
-
-    EB[...] = jnp.zeros(EB.shape, f32)
 
     def store_rates(level, D, W, RT):
         def store(z1, k1, s):
@@ -337,11 +411,32 @@
             out.append((centre[k], s))
         return out
 
-    def sweep0(dst, src):
-        def body(z):
-            for k, (c, s) in enumerate(neighbours(src, z + 1, 8, 32, 8)):
-                dst[z + 1, k, 8:40, :] = (1.0 - OMEGA) * c + W0[z, k] * (F0[z, k] + s)
-        loop(32, body)
+    def plane0(dst, src, z):
+        for x in range(4):
+            at = pl.ds(8 * x, 8)
+            for k, (c, s) in enumerate(neighbours(src, z + 1, 8 + 8 * x, 8, 8)):
+                dst[z + 1, k, pl.ds(8 + 8 * x, 8), :] = (1.0 - OMEGA) * c + W0[z, k, at, :] * (F0[z, k, at, :] + s)
+
+    def sweep0(dst, src, taking, sending, store=None):
+        if taking is not None:
+            taking.take_x(0)
+        loop(15, lambda i: plane0(dst, src, i + 1))
+        if taking is not None:
+            taking.take_z()
+            taking.take_x(1)
+        plane0(dst, src, 0)
+        if store is not None:
+            store(0)
+        else:
+            sending.send_x(0)
+        plane0(dst, src, 31)
+        if store is None:
+            sending.send_z()
+        loop(15, lambda i: plane0(dst, src, i + 16))
+        if store is not None:
+            store(1)
+        else:
+            sending.send_x(1)
 
     def sweep(level, dst, src, F, W, reach, inside=False):
         nk, n, xo, nx = NK[level], NR[level], XO[level], NX[level]
@@ -366,10 +461,12 @@
         loop(NZ[level] + 2 * HALO[level], body)
 
     def residual0(z):
-        out = []
-        for k, (c, s) in enumerate(neighbours(V2, z + 1, 8, 32, 8)):
-            d = (1.0 + 6.0 * KAPPA[0]) / KAPPA[0] + (1.0 / KAPPA[0]) * U0[z, k]
-            out.append(F0[z, k] - d * c + s)
+        out = [[] for _ in range(8)]
+        for x in range(4):
+            at = pl.ds(8 * x, 8)
+            for k, (c, s) in enumerate(neighbours(V2, z + 1, 8 + 8 * x, 8, 8)):
+                d = (1.0 + 6.0 * KAPPA[0]) / KAPPA[0] + (1.0 / KAPPA[0]) * U0[z, k, at, :]
+                out[k].append(F0[z, k, at, :] - d * c + s)
         return out
 
     def residual(level, ref, F, D):
@@ -382,12 +479,12 @@
             ]
         return plane
 
-    def coarse_source(level, plane, F, first):
+    def coarse_source(level, plane, F, first, halves=None):
         def planes(z1):
-            return [a + b for a, b in zip(plane(2 * z1), plane(2 * z1 + 1))]
+            return jax.tree.map(lambda a, b: a + b, plane(2 * z1), plane(2 * z1 + 1))
         def store(z1, k1, s):
             F[ZO[level + 1] + z1, k1, pl.ds(XO[level + 1], NX[level + 1]), :] = 0.5 * s
-        restrict(level, planes, store, first)
+        restrict(level, planes, store, first, halves)
 
     def prolong(level, dst, src, reach, rows):
         c = level + 1
@@ -421,19 +518,23 @@
                         dst[z + dz, k, pl.ds(lo_r, n_r), :] = dst[z + dz, k, pl.ds(lo_r, n_r), :] + p
         loop(NZ[c] + 2, body)
 
-    x_dens.wait_recv()
-    level0_sends = [x_dens]
-    sweep0(V1, V0)
-    x = send(0, V1, 1, FACES)
-    level0_sends.append(x)
-    for c in supply_out:
-        c.wait()
-    x.wait_recv()
-    sweep0(V2, V1)
-    x = send(0, V2, 1, FACES)
-    level0_sends.append(x)
-    x.wait_recv()
-    coarse_source(0, residual0, F1, 0)
+    def all_supply():
+        for c in supply_out:
+            c.wait()
+
+    sweep0(V1, V0, faces[0], faces[1])
+    all_supply()
+    sweep0(V2, V1, faces[1], faces[2])
+
+    def halves(gather):
+        faces[2].take_x(0)
+        loop(7, lambda i: gather(i + 1))
+        faces[2].take_z()
+        faces[2].take_x(1)
+        gather(0)
+        loop(8, lambda i: gather(i + 8))
+
+    coarse_source(0, residual0, F1, 0, halves)
 
     x = send(1, F1, HALO[1], AROUND)
     x_w1.wait_recv()
@@ -469,21 +570,26 @@
     x = send(1, C1, 1, FACES)
     x.wait_recv()
 
-    for e in level0_sends:
-        e.wait_send()
-        started.remove(e)
+    for f in faces[:3]:
+        for e in [f.z] + f.x:
+            e.wait_send()
+            started.remove(e)
     prolong(0, V2, C1, 1, (0, 48))
-    sweep0(V0, V2)
-    x = send(0, V0, 1, FACES)
-    x.wait_recv()
-    sweep0(V1, V0)
+    sweep0(V0, V2, None, faces[3])
     result_out = []
-    for k in range(8):
-        c = pltpu.make_async_copy(
-            V1.at[pl.ds(1, 32), k, pl.ds(8, 32), :], out_c.at[:, :, pl.ds(k * LANES, LANES)], out_sem.at[8 + k]
-        )
-        c.start()
-        result_out.append(c)
+
+    def store_result(half):
+        for k in range(8):
+            zs = pl.ds(16 * half, 16)
+            c = pltpu.make_async_copy(
+                V1.at[pl.ds(16 * half + 1, 16), k, pl.ds(8, 32), :],
+                out_c.at[zs, :, pl.ds(k * LANES, LANES)],
+                out_sem.at[8 + 8 * half + k],
+            )
+            c.start()
+            result_out.append(c)
+
+    sweep0(V1, V0, faces[3], None, store_result)
     for e in started:
         e.wait_send()
     for c in result_out:
@@ -510,7 +616,9 @@
         vmem(9, 8, LANES, dtype=jnp.int32), vmem(9, 8, LANES, dtype=jnp.int32),
         vmem(9 * LANES, LANES, dtype=jnp.int32),
         vmem(9 * LANES, 256, dtype=bf16), vmem(256, 256),
-        pltpu.SemaphoreType.DMA((17,)), pltpu.SemaphoreType.DMA((16,)),
+        vmem(1, 2, 2, 128, LANES), vmem(1, 2, 2, 128, LANES),
+        vmem(3, 2, 2, 128, LANES, dtype=bf16), vmem(3, 2, 2, 128, LANES, dtype=bf16),
+        pltpu.SemaphoreType.DMA((17,)), pltpu.SemaphoreType.DMA((24,)),
         pltpu.SemaphoreType.DMA((100,)), pltpu.SemaphoreType.DMA((100,)),
     ]
     return v

time: 117 us -> 105 us (0.90)
  Pallas kernels: 109 us -> 97 us
    pallas_call x1, Pallas kernels: 109 us -> 97 us  [shards(): pl.pallas_call(kernel, out_shape=(jax.ShapeDtypeStruct(density.shape, f32...]
where the time goes in v2:
time: 105 us
  Pallas kernels  97 us (92%)
  local copies, waits for them, and re-layouts  6.96 us (7%)
    pallas_call x1, Pallas kernels, shards(): pl.pallas_call(kernel, out_shape=(jax.ShapeDtypeStruct(density.shape, f32...  97 us
    unnamed x4, local copies, waits for them, and re-layouts  6.96 us

profile of v2, /device:TPU:30, one launch (start us, length us, event | category | flops | bytes accessed | tf_op | source)
XLA Modules:
  0.0 104.6 jit_solution(4501940493804818776)
XLA Ops:
  0.6 97.0 %tissue_step.1 = (f32[32,32,1024]{2,1,0:T(8,128)}, f32[32,32,1024]{2,1,0:T(8,128)}) custom-call(f32[32,32,1024]{2,1,0:T(8,128)} %dens.1, f32[32,32,1024]{2,1,0:T(8,128)} %upt.1, bf16[72,4096]{1,0:T(8,128)(2,1)} %bricks.1, s32[72]{0:T(128)} %ids.1, s32[1,9]{1,0:T(1,128)} %counts.1), custom_call_target="tpu_custom_call" | custom-call | tf_op jit(solution)/shard_map/tissue_step/pallas_call | solution.py:630
  97.6 0.0 copy-start
  97.6 4.9 %copy.9 = f32[32,32,1024]{2,1,0:T(8,128)} copy(f32[32,32,1024]{2,1,0:T(8,128)} %get-tuple-element.4) | data formatting | bytes 8388608
  102.6 0.0 copy-done
  102.6 2.0 %copy.10 = f32[32,32,1024]{2,1,0:T(8,128)} copy(f32[32,32,1024]{2,1,0:T(8,128)S(1)} %copy-done) | data formatting | bytes 8388608
Async XLA Ops:
  97.6 5.0 %copy-start = (f32[32,32,1024]{2,1,0:T(8,128)S(1)}, f32[32,32,1024]{2,1,0:T(8,128)}, u32[]{:S(2)}) copy-start(f32[32,32,1024]{2,1,0:T(8,128)} %get-tuple-element.5) | copy-start | bytes 12582916

commit v3 on v2

--- a/solution.py
+++ b/solution.py
@@ -15,14 +15,17 @@
 NZ = (32, 16, 8, 4)
 NX = (32, 16, 8, 4)
 NK = (8, 4, 2, 1)
-HALO = (1, 3, 3, 4)
-NR = (32, 24, 16, 16)
-ZO = (1, 4, 4, 5)
-XO = (8, 11, 11, 12)
-ROWS = (48, 40, 32, 32)
+HALO = (1, 4, 5, 5)
+NR = (32, 24, 24, 16)
+ZO = (1, 5, 6, 6)
+XO = (8, 12, 13, 13)
+ROWS = (48, 40, 40, 32)
 PLANES = tuple(n + 2 * o for n, o in zip(NZ, ZO))
 
 FACES = ((-1, 0), (1, 0), (0, -1), (0, 1))
+FAR = ((-2, 0), (2, 0), (0, -2), (0, 2)) + tuple(
+    (a * sz, b * sx) for a, b in ((1, 2), (2, 1)) for sz in (-1, 1) for sx in (-1, 1)
+)
 AROUND = tuple((dz, dx) for dz in (-1, 0, 1) for dx in (-1, 0, 1) if dz or dx)
 
 f32 = jnp.float32
@@ -36,11 +39,11 @@
 def kernel(
     dens, upt, bricks, ids, counts, out_s, out_c,
     V0, V1, V2, F0, W0, U0,
-    F1, W1, D1, A1, B1, C1,
-    F2, W2, D2, A2, B2, C2,
+    F1, W1, D1, A1, B1,
+    F2, W2, D2, A2, B2,
     F3, W3, A3, B3,
-    RT1, RT2, RS, EB, PB, PM, EM,
-    BV, XA, XT, VS, VR, IS, IR, RK, MB, TB,
+    RT1, RT2, EB, PM, EM,
+    BV, XX, VS, VR, IS, IR, RK, MB, TB,
     XSD, XD, XSV, XV,
     load_sem, out_sem, send_sem, recv_sem,
 ):
@@ -59,6 +62,7 @@
         return ok
 
     def loop(n, body, unroll=1):
+        unroll = max(u for u in range(1, unroll + 1) if n % u == 0)
         def step(i, c):
             body(i)
             return c
@@ -100,9 +104,10 @@
         def cut(d, first, n):
             if d == 0:
                 return (first, n), (first, n)
+            w = min(width, n) if abs(d) == 1 else width - n
             if d > 0:
-                return (first + n - width, width), (first - width, width)
-            return (first, width), (first + n, width)
+                return (first + n - w, w), (first - (d - 1) * n - w, w)
+            return (first, w), (first - d * n, w)
 
         parts = []
         for dz, dx in directions:
@@ -171,8 +176,8 @@
         return copies
 
     brick_load = pltpu.make_async_copy(bricks, BV, load_sem.at[16])
+    dens_loads = load(dens, lambda k: V0.at[pl.ds(1, 32), k, pl.ds(8, 32), :], 0)
     brick_load.start()
-    dens_loads = load(dens, lambda k: V0.at[pl.ds(1, 32), k, pl.ds(8, 32), :], 0)
     upt_loads = load(upt, lambda k: U0.at[:, k], 8)
 
     def clear(ref):
@@ -181,11 +186,11 @@
             ref[i] = jnp.zeros(shape, ref.dtype)
         loop(ref.shape[0], body)
 
-    for ref in (F1, W1, C1, F2, W2, C2, F3, W3):
+    for ref in (F1, W1, F2, W2, F3, W3):
         clear(ref)
 
     barrier = pltpu.get_barrier_semaphore()
-    for d in AROUND:
+    for d in AROUND + FAR:
         @pl.when(exists(*d))
         def _(d=d):
             pl.semaphore_signal(
@@ -218,8 +223,7 @@
             def guard(z, ref=ref, end=8 + NR[level], shape=shape):
                 ref[z, :, 0:8, :] = jnp.zeros(shape, f32)
                 ref[z, :, end : end + 8, :] = jnp.zeros(shape, f32)
-            loop(PLANES[level], guard)
-    PB[...] = jnp.zeros(PB.shape, f32)
+            loop(PLANES[level], guard, 2)
 
     row = lax.broadcasted_iota(jnp.int32, (256, LANES), 0)
     col = lax.broadcasted_iota(jnp.int32, (256, LANES), 1)
@@ -232,6 +236,16 @@
     EM[0:128] = twice
     EM[128:256] = twice
 
+    pl.semaphore_wait(barrier, sum(jnp.where(exists(*d), 1, 0) for d in AROUND + FAR))
+    for c in dens_loads:
+        c.wait()
+    faces = [Faces(V0, XSD.at[0], XD.at[0])]
+    for e, V in enumerate((V1, V2, V0)):
+        faces.append(Faces(V, XSV.at[e], XV.at[e]))
+    faces[0].send_z()
+    for half in range(2):
+        faces[0].send_x(half)
+
     for j in range(9):
         for e in range(CAP):
             IS[j, e : e + 1, :] = jnp.full((1, LANES), ids[CAP * j + e], jnp.int32)
@@ -246,13 +260,13 @@
     def widen(k):
         v = BV[:, pl.ds(pl.multiple_of(k * LANES, LANES), LANES)].astype(f32)
         for j in range(9):
-            XA[pl.ds(pl.multiple_of((j * 32 + k) * 8, 8), 8), :] = v[8 * j : 8 * j + 8]
-
-    loop(32, widen, unroll=2)
+            XX[pl.ds(pl.multiple_of((j * 32 + k) * 8, 8), 8), :] = v[8 * j : 8 * j + 8]
+
+    loop(32, widen, 4)
     chunk = lax.broadcasted_iota(jnp.int32, (32, LANES), 1) // 16
 
     def regroup(j):
-        xs = [XA[pl.ds(j * 256 + s, 32, stride=8), :] for s in range(8)]
+        xs = [XX[pl.ds(j * 256 + s, 32, stride=8), :] for s in range(8)]
         for p in (1, 2, 4):
             low = (chunk & p) == 0
             for s in range(8):
@@ -261,17 +275,12 @@
                     xs[s] = jnp.where(low, a, pltpu.roll(b, 16 * p, 1))
                     xs[s | p] = jnp.where(low, pltpu.roll(a, LANES - 16 * p, 1), b)
         for t in range(8):
-            XT[pl.ds(j * 256 + t, 32, stride=8), :] = xs[t]
-        VS[j] = XT[pl.ds(pl.multiple_of(j * 256, 256), 256), :].astype(bf16)
-
-    loop(9, regroup)
+            XX[pl.ds(2304 + j * 256 + t, 32, stride=8), :] = xs[t]
+        VS[j] = XX[pl.ds(pl.multiple_of(2304 + j * 256, 256), 256), :].astype(bf16)
+
+    loop(9, regroup, 3)
     VR[:, 4 * LANES : 5 * LANES] = VS[4]
     IR[4] = IS[4]
-
-    def beside(at, n):
-        return 1 + jnp.where(at > 0, 1, 0) + jnp.where(at < n - 1, 1, 0)
-
-    pl.semaphore_wait(barrier, beside(gz, nz_dev) * beside(xy, nx_dev) - 1)
 
     parts = []
     for dz, dx in AROUND:
@@ -288,15 +297,6 @@
         started.append(e)
         return e
 
-    for c in dens_loads:
-        c.wait()
-    faces = [Faces(V0, XSD.at[0], XD.at[0])]
-    for e, V in enumerate((V1, V2, V0)):
-        faces.append(Faces(V, XSV.at[e], XV.at[e]))
-    faces[0].send_z()
-    for half in range(2):
-        faces[0].send_x(half)
-
     for c in upt_loads:
         c.wait()
 
@@ -304,7 +304,7 @@
         for k in range(8):
             W0[z, k] = (OMEGA * KAPPA[0]) / (1.0 + 6.0 * KAPPA[0] + U0[z, k])
 
-    loop(32, weights0)
+    loop(32, weights0, 2)
 
     def split(x):
         hi = x.astype(bf16)
@@ -313,18 +313,23 @@
     def restrict(level, planes, store, first, halves=None):
         rows = NX[level] // 2
         step = max(8, rows)
+        nk, half = NK[level], NZ[level] // 2
         def gather(z1):
             for k, v in enumerate(planes(z1)):
                 v = v if isinstance(v, list) else [v]
                 n = v[0].shape[0]
                 for x, part in enumerate(v):
-                    RS[k, x * n : (x + 1) * n, :] = part
-                s = RS[k, pl.ds(first, rows, stride=2), :] + RS[k, pl.ds(first + 1, rows, stride=2), :]
-                EB[k // 2, k % 2, pl.ds(pl.multiple_of(z1 * step, step), rows), :] = s
+                    XX[pl.ds(pl.multiple_of((z1 * nk + k) * 32 + x * n, 8), n), :] = part
         if halves is None:
-            loop(NZ[level] // 2, gather)
+            loop(half, gather, 2 if level == 0 else 4)
         else:
             halves(gather)
+        def pair(z1):
+            for k in range(nk):
+                at = (z1 * nk + k) * 32 + first
+                s = XX[pl.ds(at, rows, stride=2), :] + XX[pl.ds(at + 1, rows, stride=2), :]
+                EB[k // 2, k % 2, pl.ds(pl.multiple_of(z1 * step, step), rows), :] = s
+        loop(half, pair, 4)
         n = NZ[level] // 2 * step
         for k1 in range(NK[level] // 2):
             x = jnp.concatenate([EB[k1, 0, 0:n, :], EB[k1, 1, 0:n, :]], axis=1)
@@ -351,7 +356,7 @@
     restrict(2, lambda z1: [RT2[2 * z1, k] + RT2[2 * z1 + 1, k] for k in range(2)], store_rates(3, None, W3, None), 0)
     x_w1 = send(1, W1, HALO[1], AROUND)
     x_w2 = send(2, W2, HALO[2], AROUND)
-    x_w3 = send(3, W3, HALO[3], AROUND)
+    x_w3 = send(3, W3, HALO[3], AROUND + FAR)
 
     send_bricks.wait_recv()
     inner = lax.broadcasted_iota(jnp.int32, (16, LANES), 0)
@@ -361,7 +366,7 @@
             r = jnp.broadcast_to(IR[j, s : s + 1, :], (16, LANES))
             RK[pl.ds(pl.multiple_of(j * 128 + s * 16, 16), 16), :] = jnp.where(r < 0, -1, r * 16 + inner)
 
-    loop(9, keys)
+    loop(9, keys, 3)
     lane = lax.broadcasted_iota(jnp.int32, (LANES, LANES), 1)
 
     def secrete(i):
@@ -371,7 +376,7 @@
             for half in range(2):
                 hit = key == lane + (i * 256 + half * 128)
                 MB[at, half * 128 : half * 128 + 128] = jnp.where(hit, 1.0, 0.0).astype(bf16)
-        loop(9, one_hot)
+        loop(9, one_hot, 3)
         TB[...] = jnp.dot(VR[...], MB[...], preferred_element_type=f32)
         g = i // 4
         bz, bx, kk = g // 2, g % 2, i % 4
@@ -420,7 +425,7 @@
     def sweep0(dst, src, taking, sending, store=None):
         if taking is not None:
             taking.take_x(0)
-        loop(15, lambda i: plane0(dst, src, i + 1))
+        loop(15, lambda i: plane0(dst, src, i + 1), 5)
         if taking is not None:
             taking.take_z()
             taking.take_x(1)
@@ -432,24 +437,20 @@
         plane0(dst, src, 31)
         if store is None:
             sending.send_z()
-        loop(15, lambda i: plane0(dst, src, i + 16))
+        loop(15, lambda i: plane0(dst, src, i + 16), 5)
         if store is not None:
             store(1)
         else:
             sending.send_x(1)
 
-    def sweep(level, dst, src, F, W, reach, inside=False):
-        nk, n, xo, nx = NK[level], NR[level], XO[level], NX[level]
+    def sweep(level, dst, src, F, W, reach):
+        nk, n = NK[level], NR[level]
         start = ZO[level] - reach
         def body(i):
             z = start + i
             for k, (c, s) in enumerate(neighbours(src, z, 8, n, nk)):
-                v = (1.0 - OMEGA) * c + W[z, k, 8 : 8 + n, :] * (F[z, k, 8 : 8 + n, :] + s)
-                if inside:
-                    dst[z, k, xo : xo + nx, :] = v[xo - 8 : xo - 8 + nx]
-                else:
-                    dst[z, k, 8 : 8 + n, :] = v
-        loop(NZ[level] + 2 * reach, body)
+                dst[z, k, 8 : 8 + n, :] = (1.0 - OMEGA) * c + W[z, k, 8 : 8 + n, :] * (F[z, k, 8 : 8 + n, :] + s)
+        loop(NZ[level] + 2 * reach, body, 8)
 
     def from_zero(level, dst, F, W):
         n = NR[level]
@@ -458,7 +459,7 @@
             z = start + i
             for k in range(NK[level]):
                 dst[z, k, 8 : 8 + n, :] = W[z, k, 8 : 8 + n, :] * F[z, k, 8 : 8 + n, :]
-        loop(NZ[level] + 2 * HALO[level], body)
+        loop(NZ[level] + 2 * HALO[level], body, 4)
 
     def residual0(z):
         out = [[] for _ in range(8)]
@@ -486,37 +487,33 @@
             F[ZO[level + 1] + z1, k1, pl.ds(XO[level + 1], NX[level + 1]), :] = 0.5 * s
         restrict(level, planes, store, first, halves)
 
-    def prolong(level, dst, src, reach, rows):
+    def prolong(level, dst, src, reach, buf, block):
         c = level + 1
-        n = NR[c]
+        n, nk = NR[c], NK[level]
         base = XO[level] + 2 * (8 - XO[c])
-        first = ZO[c] - 1
-        def body(i):
-            zc = first + i
-            x = jnp.concatenate([src[zc, k, 8 : 8 + n, :] for k in range(NK[c])], axis=0)
-            hi, lo = split(x)
-            y = jnp.dot(jnp.concatenate([hi, lo], axis=1), EM[...], preferred_element_type=f32)
-            for k in range(NK[level]):
+        first, count = ZO[c] - reach, NZ[c] + 2 * reach
+        def spread(i):
+            x = jnp.concatenate([src[first + i, k, 8 : 8 + n, :] for k in range(NK[c])], axis=0)
+            y = jnp.dot(jnp.concatenate(split(x), axis=1), EM[...], preferred_element_type=f32)
+            for k in range(nk):
                 v = y[(k // 2) * n : (k // 2 + 1) * n, (k % 2) * 128 : (k % 2 + 1) * 128]
-                PB[k, pl.ds(base, n, stride=2), :] = v
-                PB[k, pl.ds(base + 1, n, stride=2), :] = v
-            z = ZO[level] + 2 * (zc - ZO[c])
-            lo_r, n_r = rows
-            if level == 0:
-                for k in range(NK[level]):
-                    p = PB[k, pl.ds(lo_r, n_r), :]
-                    @pl.when(i > 0)
-                    def _():
-                        dst[z, k, pl.ds(lo_r, n_r), :] = dst[z, k, pl.ds(lo_r, n_r), :] + p
-                    @pl.when(i < NZ[c] + 1)
-                    def _():
-                        dst[z + 1, k, pl.ds(lo_r, n_r), :] = dst[z + 1, k, pl.ds(lo_r, n_r), :] + p
-            else:
-                for k in range(NK[level]):
-                    p = PB[k, pl.ds(lo_r, n_r), :]
-                    for dz in range(2):
-                        dst[z + dz, k, pl.ds(lo_r, n_r), :] = dst[z + dz, k, pl.ds(lo_r, n_r), :] + p
-        loop(NZ[c] + 2, body)
+                at = (i * nk + k) * block + base
+                buf[pl.ds(at, n, stride=2), :] = v
+                buf[pl.ds(at + 1, n, stride=2), :] = v
+        loop(count, spread, 4)
+        low, rows = (0, 48) if level == 0 else (8, NR[level])
+        def add(i, which=(0, 1)):
+            z = ZO[level] + 2 * (i - reach)
+            for k in range(nk):
+                p = buf[pl.ds(pl.multiple_of((i * nk + k) * block + low, 8), rows), :]
+                for dz in which:
+                    dst[z + dz, k, low : low + rows, :] = dst[z + dz, k, low : low + rows, :] + p
+        if level == 0:
+            add(0, (1,))
+            loop(count - 2, lambda i: add(i + 1), 2)
+            add(count - 1, (0,))
+        else:
+            loop(count, add, 2)
 
     def all_supply():
         for c in supply_out:
@@ -528,11 +525,12 @@
 
     def halves(gather):
         faces[2].take_x(0)
-        loop(7, lambda i: gather(i + 1))
+        loop(6, lambda i: gather(i + 1), 3)
         faces[2].take_z()
         faces[2].take_x(1)
         gather(0)
-        loop(8, lambda i: gather(i + 8))
+        gather(7)
+        loop(8, lambda i: gather(i + 8), 4)
 
     coarse_source(0, residual0, F1, 0, halves)
 
@@ -540,41 +538,37 @@
     x_w1.wait_recv()
     x.wait_recv()
     from_zero(1, A1, F1, W1)
-    sweep(1, B1, A1, F1, W1, 2)
+    sweep(1, B1, A1, F1, W1, 3)
     coarse_source(1, residual(1, B1, F1, D1), F2, XO[1] - 8)
 
     x = send(2, F2, HALO[2], AROUND)
     x_w2.wait_recv()
     x.wait_recv()
     from_zero(2, A2, F2, W2)
-    sweep(2, B2, A2, F2, W2, 2)
+    sweep(2, B2, A2, F2, W2, 4)
     coarse_source(2, residual(2, B2, F2, D2), F3, XO[2] - 8)
 
-    x = send(3, F3, HALO[3], AROUND)
+    x = send(3, F3, HALO[3], AROUND + FAR)
     x_w3.wait_recv()
     x.wait_recv()
     from_zero(3, A3, F3, W3)
-    sweep(3, B3, A3, F3, W3, 3)
-    sweep(3, A3, B3, F3, W3, 2)
-    sweep(3, B3, A3, F3, W3, 1)
-
-    prolong(2, B2, B3, 1, (8, NR[2]))
-    sweep(2, A2, B2, F2, W2, 1)
-    sweep(2, C2, A2, F2, W2, 0, inside=True)
-    x = send(2, C2, 1, AROUND)
-    x.wait_recv()
-
-    prolong(1, B1, C2, 1, (8, NR[1]))
-    sweep(1, A1, B1, F1, W1, 1)
-    sweep(1, C1, A1, F1, W1, 0, inside=True)
-    x = send(1, C1, 1, FACES)
-    x.wait_recv()
+    sweep(3, B3, A3, F3, W3, 4)
+    sweep(3, A3, B3, F3, W3, 3)
+    sweep(3, B3, A3, F3, W3, 2)
+
+    prolong(2, B2, B3, 2, XX, 64)
+    sweep(2, A2, B2, F2, W2, 3)
+    sweep(2, B2, A2, F2, W2, 2)
+
+    prolong(1, B1, B2, 2, XX, 64)
+    sweep(1, A1, B1, F1, W1, 2)
+    sweep(1, B1, A1, F1, W1, 1)
 
     for f in faces[:3]:
         for e in [f.z] + f.x:
             e.wait_send()
             started.remove(e)
-    prolong(0, V2, C1, 1, (0, 48))
+    prolong(0, V2, B1, 1, faces[1].rows, 48)
     sweep0(V0, V2, None, faces[3])
     result_out = []
 
@@ -602,16 +596,14 @@
 
     v = [vmem(*level_shape(0)) for _ in range(3)]
     v += [vmem(32, 8, 32, LANES) for _ in range(3)]
-    for level, count in ((1, 6), (2, 6), (3, 4)):
+    for level, count in ((1, 5), (2, 5), (3, 4)):
         v += [vmem(*level_shape(level)) for _ in range(count)]
     v += [
         vmem(16, 4, 16, LANES), vmem(8, 2, 8, LANES),
-        vmem(8, 32, LANES),
         vmem(4, 2, 256, LANES),
-        vmem(8, 56, LANES),
         vmem(512, LANES, dtype=bf16), vmem(256, 256, dtype=bf16),
         vmem(SLOTS, BRICK, dtype=bf16),
-        vmem(9 * 256, LANES), vmem(9 * 256, LANES),
+        vmem(18 * 256, LANES),
         vmem(9, 256, LANES, dtype=bf16), vmem(256, 9 * LANES, dtype=bf16),
         vmem(9, 8, LANES, dtype=jnp.int32), vmem(9, 8, LANES, dtype=jnp.int32),
         vmem(9 * LANES, LANES, dtype=jnp.int32),
@@ -619,7 +611,7 @@
         vmem(1, 2, 2, 128, LANES), vmem(1, 2, 2, 128, LANES),
         vmem(3, 2, 2, 128, LANES, dtype=bf16), vmem(3, 2, 2, 128, LANES, dtype=bf16),
         pltpu.SemaphoreType.DMA((17,)), pltpu.SemaphoreType.DMA((24,)),
-        pltpu.SemaphoreType.DMA((100,)), pltpu.SemaphoreType.DMA((100,)),
+        pltpu.SemaphoreType.DMA((120,)), pltpu.SemaphoreType.DMA((120,)),
     ]
     return v
 

time: 105 us -> 85.8 us (0.82)
  Pallas kernels: 97 us -> 77.2 us
    pallas_call x1, Pallas kernels: 97 us -> 77.2 us  [shards(): pl.pallas_call(kernel, out_shape=(jax.ShapeDtypeStruct(density.shape, f32...]
where the time goes in v3:
time: 85.8 us; the launch traced here: 84.8 us
  Pallas kernels  77.2 us (90%)
  local copies, waits for them, and re-layouts  6.96 us (8%)
    pallas_call x1, Pallas kernels, shards(): pl.pallas_call(kernel, out_shape=(jax.ShapeDtypeStruct(density.shape, f32...  77.2 us
    unnamed x4, local copies, waits for them, and re-layouts  6.96 us

profile of v3, /device:TPU:30, one launch (start us, length us, event | category | flops | bytes accessed | tf_op | source)
XLA Modules:
  0.0 84.8 jit_solution(9344647540475033886)
XLA Ops:
  0.6 77.2 %tissue_step.1 = (f32[32,32,1024]{2,1,0:T(8,128)}, f32[32,32,1024]{2,1,0:T(8,128)}) custom-call(f32[32,32,1024]{2,1,0:T(8,128)} %dens.1, f32[32,32,1024]{2,1,0:T(8,128)} %upt.1, bf16[72,4096]{1,0:T(8,128)(2,1)} %bricks.1, s32[72]{0:T(128)} %ids.1, s32[1,9]{1,0:T(1,128)} %counts.1), custom_call_target="tpu_custom_call" | custom-call | tf_op jit(solution)/shard_map/tissue_step/pallas_call | solution.py:622
  77.9 0.0 copy-start
  77.9 4.9 %copy.9 = f32[32,32,1024]{2,1,0:T(8,128)} copy(f32[32,32,1024]{2,1,0:T(8,128)} %get-tuple-element.4) | data formatting | bytes 8388608
  82.8 0.0 copy-done
  82.8 2.0 %copy.10 = f32[32,32,1024]{2,1,0:T(8,128)} copy(f32[32,32,1024]{2,1,0:T(8,128)S(1)} %copy-done) | data formatting | bytes 8388608
Async XLA Ops:
  77.9 5.0 %copy-start = (f32[32,32,1024]{2,1,0:T(8,128)S(1)}, f32[32,32,1024]{2,1,0:T(8,128)}, u32[]{:S(2)}) copy-start(f32[32,32,1024]{2,1,0:T(8,128)} %get-tuple-element.5) | copy-start | bytes 12582916

commit v4 on v3

--- a/solution.py
+++ b/solution.py
@@ -43,8 +43,8 @@
     F2, W2, D2, A2, B2,
     F3, W3, A3, B3,
     RT1, RT2, EB, PM, EM,
-    BV, XX, VS, VR, IS, IR, RK, MB, TB,
-    XSD, XD, XSV, XV,
+    BV, XX, VS, VR, VG, IS, IR, RK, MB, TB,
+    XSD, XD, XSV, XV, PK, LK,
     load_sem, out_sem, send_sem, recv_sem,
 ):
     gz, xy = lax.axis_index("gz"), lax.axis_index("xy")
@@ -165,6 +165,41 @@
         def take_z(self):
             self.z.wait_recv()
 
+    class Strips:
+        def __init__(self, ref, out, into):
+            self.flat = ref.reshape(PLANES[1] * NK[1] * ROWS[1], LANES)
+            self.out, self.into = out, into
+            self.planes = halo_exchange(1, ref, HALO[1], ((-1, 0), (1, 0)))
+            self.cuts = []
+            for dz, src, dst in ((-1, (0, 16), (80, 16)), (0, (0, 64), (16, 64)), (1, (48, 16), (0, 16))):
+                for side, dx in ((0, -1), (1, 1)):
+                    self.cuts.append(((dz, dx), side, pl.ds(*src), pl.ds(*dst)))
+            self.rows = Exchange([
+                (d, out.at[side, :, src, :], into.at[side, :, dst, :]) for d, side, src, dst in self.cuts
+            ])
+
+        def clear(self):
+            for d, side, _, dst in self.cuts:
+                @pl.when(absent(-d[0], -d[1]))
+                def _(side=side, dst=dst):
+                    self.into[side, :, dst, :] = jnp.zeros((4, dst.size, LANES), bf16)
+
+        def send(self):
+            for side, x in ((0, XO[1]), (1, XO[1] + 12)):
+                for r in range(4):
+                    v = self.flat[pl.ds(ZO[1] * 160 + x + r, 64, stride=40), :]
+                    self.out[side, r] = v.astype(bf16)
+            for e in (self.rows, self.planes):
+                e.start()
+                started.append(e)
+
+        def take(self):
+            self.planes.wait_recv()
+            self.rows.wait_recv()
+            for side, x in ((0, XO[1] + 16), (1, XO[1] - 4)):
+                for r in range(4):
+                    self.flat[pl.ds((ZO[1] - 4) * 160 + x + r, 96, stride=40), :] = self.into[side, r].astype(f32)
+
     def load(src, dst_of, base):
         copies = []
         for k in range(8):
@@ -216,7 +251,10 @@
         @pl.when(absent(*d))
         def _(j=j):
             VR[:, j * LANES : (j + 1) * LANES] = jnp.zeros((256, LANES), bf16)
-            IR[j] = jnp.full((CAP, LANES), -1, jnp.int32)
+            IR[j] = jnp.full((2 * CAP, LANES), -1, jnp.int32)
+    strips_w, strips_f = Strips(W1, PK.at[0], LK.at[0]), Strips(F1, PK.at[1], LK.at[1])
+    strips_w.clear()
+    strips_f.clear()
     for level, refs in ((1, (A1, B1)), (2, (A2, B2)), (3, (A3, B3))):
         shape = (NK[level], 8, LANES)
         for ref in refs:
@@ -236,7 +274,25 @@
     EM[0:128] = twice
     EM[128:256] = twice
 
+    slot = lax.broadcasted_iota(jnp.int32, (CAP, LANES), 0)
+    here = slot == lax.broadcasted_iota(jnp.int32, (CAP, LANES), 1) // 16
+    for j in range(9):
+        for e in range(CAP):
+            IS[j, e : e + 1, :] = jnp.full((1, LANES), ids[CAP * j + e], jnp.int32)
+    for j in range(9):
+        v = IS[j, 0:8, :]
+        v = (((v >> 11) & 1) * 2 + ((v >> 6) & 1)) * 64 + (v & 63)
+        v = jnp.where(slot < counts[0, j], v, -1)
+        IS[j, 0:8, :] = v
+        IS[j, 8:16, :] = jnp.broadcast_to(jnp.sum(jnp.where(here, v, 0), axis=0, keepdims=True), (CAP, LANES))
+    IR[4] = IS[4]
+
     pl.semaphore_wait(barrier, sum(jnp.where(exists(*d), 1, 0) for d in AROUND + FAR))
+    send_ids = Exchange([
+        ((dz, dx), IS.at[(dz + 1) * 3 + dx + 1], IR.at[(dz + 1) * 3 + dx + 1]) for dz, dx in AROUND
+    ])
+    send_ids.start()
+    started.append(send_ids)
     for c in dens_loads:
         c.wait()
     faces = [Faces(V0, XSD.at[0], XD.at[0])]
@@ -245,15 +301,6 @@
     faces[0].send_z()
     for half in range(2):
         faces[0].send_x(half)
-
-    for j in range(9):
-        for e in range(CAP):
-            IS[j, e : e + 1, :] = jnp.full((1, LANES), ids[CAP * j + e], jnp.int32)
-    slot = lax.broadcasted_iota(jnp.int32, (CAP, LANES), 0)
-    for j in range(9):
-        v = IS[j]
-        local = (((v >> 11) & 1) * 2 + ((v >> 6) & 1)) * 64 + (v & 63)
-        IS[j] = jnp.where(slot < counts[0, j], local, -1)
 
     brick_load.wait()
 
@@ -280,13 +327,10 @@
 
     loop(9, regroup, 3)
     VR[:, 4 * LANES : 5 * LANES] = VS[4]
-    IR[4] = IS[4]
-
     parts = []
     for dz, dx in AROUND:
         j = (dz + 1) * 3 + dx + 1
         parts.append(((dz, dx), VS.at[j], VR.at[:, pl.ds(j * LANES, LANES)]))
-        parts.append(((dz, dx), IS.at[j], IR.at[j]))
     send_bricks = Exchange(parts)
     send_bricks.start()
     started.append(send_bricks)
@@ -354,44 +398,48 @@
     restrict(0, lambda z1: [U0[2 * z1, k] + U0[2 * z1 + 1, k] for k in range(8)], store_rates(1, D1, W1, RT1), 0)
     restrict(1, lambda z1: [RT1[2 * z1, k] + RT1[2 * z1 + 1, k] for k in range(4)], store_rates(2, D2, W2, RT2), 0)
     restrict(2, lambda z1: [RT2[2 * z1, k] + RT2[2 * z1 + 1, k] for k in range(2)], store_rates(3, None, W3, None), 0)
-    x_w1 = send(1, W1, HALO[1], AROUND)
+    strips_w.send()
     x_w2 = send(2, W2, HALO[2], AROUND)
     x_w3 = send(3, W3, HALO[3], AROUND + FAR)
 
+    send_ids.wait_recv()
+    inner = lax.broadcasted_iota(jnp.int32, (16, LANES), 0)
+    lane = lax.broadcasted_iota(jnp.int32, (LANES, LANES), 1)
+
+    def one_hot(j):
+        for e in range(CAP):
+            r = jnp.broadcast_to(IR[j, e : e + 1, :], (16, LANES))
+            RK[e * 16 : e * 16 + 16, :] = jnp.where(r < 0, -1, (r & 63) * 16 + inner)
+        for k in range(8):
+            hit = RK[...] == lane + k * LANES
+            at = pl.ds(pl.multiple_of(j * LANES, LANES), LANES)
+            MB[at, k * LANES : (k + 1) * LANES] = jnp.where(hit, 1.0, 0.0).astype(bf16)
+
+    loop(9, one_hot)
     send_bricks.wait_recv()
-    inner = lax.broadcasted_iota(jnp.int32, (16, LANES), 0)
-
-    def keys(j):
-        for s in range(8):
-            r = jnp.broadcast_to(IR[j, s : s + 1, :], (16, LANES))
-            RK[pl.ds(pl.multiple_of(j * 128 + s * 16, 16), 16), :] = jnp.where(r < 0, -1, r * 16 + inner)
-
-    loop(9, keys, 3)
-    lane = lax.broadcasted_iota(jnp.int32, (LANES, LANES), 1)
+    for j in range(9):
+        v = VR[:, j * LANES : (j + 1) * LANES]
+        column = IR[j, 8:9, :] >> 6
+        for g in range(4):
+            mask = jnp.broadcast_to(jnp.where(column == g, 1.0, 0.0), (256, LANES)).astype(bf16)
+            VG[g * 256 : (g + 1) * 256, j * LANES : (j + 1) * LANES] = v * mask
 
     def secrete(i):
-        def one_hot(j):
-            at = pl.ds(pl.multiple_of(j * 128, 128), 128)
-            key = RK[at, :]
+        block = MB[:, pl.ds(pl.multiple_of(i * 256, 256), 256)]
+        TB[...] = jnp.dot(VG[...], block, preferred_element_type=f32)
+        def place(q):
+            g = q // 16
+            z = g // 2 * 16 + q % 16
             for half in range(2):
-                hit = key == lane + (i * 256 + half * 128)
-                MB[at, half * 128 : half * 128 + 128] = jnp.where(hit, 1.0, 0.0).astype(bf16)
-        loop(9, one_hot, 3)
-        TB[...] = jnp.dot(VR[...], MB[...], preferred_element_type=f32)
-        g = i // 4
-        bz, bx, kk = g // 2, g % 2, i % 4
-        def place(a):
-            z = bz * 16 + a
-            for half in range(2):
-                k = 2 * kk + half
-                x = pl.multiple_of(8 + bx * 16, 8)
-                t = TB[pl.ds(pl.multiple_of(a * 16, 16), 16), half * 128 : half * 128 + 128]
-                s = V0[z + 1, k, pl.ds(x, 16), :] + t
-                V2[z + 1, k, pl.ds(x, 16), :] = s
-                F0[z, k, pl.ds(pl.multiple_of(bx * 16, 8), 16), :] = s * (1.0 / KAPPA[0])
-        loop(16, place, unroll=4)
-
-    loop(16, secrete)
+                k = 2 * i + half
+                t = TB[pl.ds(pl.multiple_of(q * 16, 16), 16), half * LANES : (half + 1) * LANES]
+                x = pl.ds(pl.multiple_of(8 + g % 2 * 16, 8), 16)
+                s = V0[z + 1, k, x, :] + t
+                V2[z + 1, k, x, :] = s
+                F0[z, k, pl.ds(pl.multiple_of(g % 2 * 16, 8), 16), :] = s * (1.0 / KAPPA[0])
+        loop(64, place, 8)
+
+    loop(4, secrete)
     supply_out = []
     for k in range(8):
         c = pltpu.make_async_copy(
@@ -534,9 +582,9 @@
 
     coarse_source(0, residual0, F1, 0, halves)
 
-    x = send(1, F1, HALO[1], AROUND)
-    x_w1.wait_recv()
-    x.wait_recv()
+    strips_f.send()
+    strips_w.take()
+    strips_f.take()
     from_zero(1, A1, F1, W1)
     sweep(1, B1, A1, F1, W1, 3)
     coarse_source(1, residual(1, B1, F1, D1), F2, XO[1] - 8)
@@ -605,11 +653,13 @@
         vmem(SLOTS, BRICK, dtype=bf16),
         vmem(18 * 256, LANES),
         vmem(9, 256, LANES, dtype=bf16), vmem(256, 9 * LANES, dtype=bf16),
-        vmem(9, 8, LANES, dtype=jnp.int32), vmem(9, 8, LANES, dtype=jnp.int32),
-        vmem(9 * LANES, LANES, dtype=jnp.int32),
-        vmem(9 * LANES, 256, dtype=bf16), vmem(256, 256),
+        vmem(1024, 9 * LANES, dtype=bf16),
+        vmem(9, 16, LANES, dtype=jnp.int32), vmem(9, 16, LANES, dtype=jnp.int32),
+        vmem(LANES, LANES, dtype=jnp.int32),
+        vmem(9 * LANES, 1024, dtype=bf16), vmem(1024, 256),
         vmem(1, 2, 2, 128, LANES), vmem(1, 2, 2, 128, LANES),
         vmem(3, 2, 2, 128, LANES, dtype=bf16), vmem(3, 2, 2, 128, LANES, dtype=bf16),
+        vmem(2, 2, 4, 64, LANES, dtype=bf16), vmem(2, 2, 4, 96, LANES, dtype=bf16),
         pltpu.SemaphoreType.DMA((17,)), pltpu.SemaphoreType.DMA((24,)),
         pltpu.SemaphoreType.DMA((120,)), pltpu.SemaphoreType.DMA((120,)),
     ]

time: 85.8 us -> 83.7 us (0.976)
  Pallas kernels: 77.2 us -> 75.1 us
    pallas_call x1, Pallas kernels: 77.2 us -> 75.1 us  [shards(): pl.pallas_call(kernel, out_shape=(jax.ShapeDtypeStruct(density.shape, f32...]
where the time goes in v4:
time: 83.7 us; the launch traced here: 82.7 us
  Pallas kernels  75.1 us (90%)
  local copies, waits for them, and re-layouts  6.96 us (8%)
    pallas_call x1, Pallas kernels, shards(): pl.pallas_call(kernel, out_shape=(jax.ShapeDtypeStruct(density.shape, f32...  75.1 us
    unnamed x4, local copies, waits for them, and re-layouts  6.96 us

profile of v4, /device:TPU:30, one launch (start us, length us, event | category | flops | bytes accessed | tf_op | source)
XLA Modules:
  0.0 82.7 jit_solution(14148497838867965083)
XLA Ops:
  0.6 75.1 %tissue_step.1 = (f32[32,32,1024]{2,1,0:T(8,128)}, f32[32,32,1024]{2,1,0:T(8,128)}) custom-call(f32[32,32,1024]{2,1,0:T(8,128)} %dens.1, f32[32,32,1024]{2,1,0:T(8,128)} %upt.1, bf16[72,4096]{1,0:T(8,128)(2,1)} %bricks.1, s32[72]{0:T(128)} %ids.1, s32[1,9]{1,0:T(1,128)} %counts.1), custom_call_target="tpu_custom_call" | custom-call | tf_op jit(solution)/shard_map/tissue_step/pallas_call | solution.py:672
  75.8 0.0 copy-start
  75.8 4.9 %copy.9 = f32[32,32,1024]{2,1,0:T(8,128)} copy(f32[32,32,1024]{2,1,0:T(8,128)} %get-tuple-element.4) | data formatting | bytes 8388608
  80.7 0.0 copy-done
  80.7 2.0 %copy.10 = f32[32,32,1024]{2,1,0:T(8,128)} copy(f32[32,32,1024]{2,1,0:T(8,128)S(1)} %copy-done) | data formatting | bytes 8388608
Async XLA Ops:
  75.8 5.0 %copy-start = (f32[32,32,1024]{2,1,0:T(8,128)S(1)}, f32[32,32,1024]{2,1,0:T(8,128)}, u32[]{:S(2)}) copy-start(f32[32,32,1024]{2,1,0:T(8,128)} %get-tuple-element.5) | copy-start | bytes 12582916
